TPU v7x, 32 devices: a whole 2x2x4 slice. The times are simulated.
32 devices in a mesh: dp: 16 (over z, x, core), exp: 2 (over y).
Axes of the slice: x: 2, y: 2, z: 4, core: 2. Of those that a mesh axis runs over, the one named last changes fastest.
Arguments:
- tokens: bfloat16 [4096, 1024], P(('dp', 'exp')), may hold values from -6 to 6
- cotangent: bfloat16 [4096, 1024], P(('dp', 'exp')), may hold values from -6 to 6
- doc_lengths: int32 [64, 3], P(('dp', 'exp')), may hold values from 1 to 48, 64 in all within a row
- routes: int32 [4096, 8], P(('dp', 'exp')), may hold values from 0 to 15, all different within a row; in each aligned block of 64 rows (0 to 63, 64 to 127, ...) at most 40 rows name the same one
- qkv_weight: float32 [1024, 2048], P(('dp', 'exp')), may hold values from -0.25 to 0.25
- qkv_mean: float32 [1024, 2048], P(('dp', 'exp')), may hold values from -128 to 128
- qkv_square: float32 [1024, 2048], P(('dp', 'exp')), may hold values from 1843.2 to 7372.8
- out_weight: float32 [1024, 1024], P(('dp', 'exp')), may hold values from -0.5 to 0.5
- out_mean: float32 [1024, 1024], P(('dp', 'exp')), may hold values from -40 to 40
- out_square: float32 [1024, 1024], P(('dp', 'exp')), may hold values from 163.84 to 655.36
- router_weight: float32 [1024, 16], P(('dp', 'exp')), may hold values from -0.09375 to 0.09375
- router_mean: float32 [1024, 16], P(('dp', 'exp')), may hold values from -512 to 512
- router_square: float32 [1024, 16], P(('dp', 'exp')), may hold values from 34816 to 139264
- norm_gains: float32 [1024, 2], P(('dp', 'exp')), may hold values from 0.5 to 1.5
- gains_mean: float32 [1024, 2], P(('dp', 'exp')), may hold values from -160 to 160
- gains_square: float32 [1024, 2], P(('dp', 'exp')), may hold values from 3276.8 to 13107.2
- in_weight: float32 [16, 1024, 1024], P('exp', 'dp'), may hold values from -0.1875 to 0.1875
- in_mean: float32 [16, 1024, 1024], P('exp', 'dp'), may hold values from -20 to 20
- in_square: float32 [16, 1024, 1024], P('exp', 'dp'), may hold values from 51.2 to 204.8
- down_weight: float32 [16, 1024, 512], P('exp', 'dp'), may hold values from -2 to 2
- down_mean: float32 [16, 1024, 512], P('exp', 'dp'), may hold values from -5 to 5
- down_square: float32 [16, 1024, 512], P('exp', 'dp'), may hold values from 0.57344 to 2.2528
Outputs:
- block_out: bfloat16 [4096, 1024], P(('dp', 'exp'))
- input_grad: bfloat16 [4096, 1024], P(('dp', 'exp'))
- new_qkv: float32 [1024, 2048], P(('dp', 'exp'))
- new_qkv_mean: float32 [1024, 2048], P(('dp', 'exp'))
- new_qkv_square: float32 [1024, 2048], P(('dp', 'exp'))
- new_out: float32 [1024, 1024], P(('dp', 'exp'))
- new_out_mean: float32 [1024, 1024], P(('dp', 'exp'))
- new_out_square: float32 [1024, 1024], P(('dp', 'exp'))
- new_router: float32 [1024, 16], P(('dp', 'exp'))
- new_router_mean: float32 [1024, 16], P(('dp', 'exp'))
- new_router_square: float32 [1024, 16], P(('dp', 'exp'))
- new_gains: float32 [1024, 2], P(('dp', 'exp'))
- new_gains_mean: float32 [1024, 2], P(('dp', 'exp'))
- new_gains_square: float32 [1024, 2], P(('dp', 'exp'))
- new_in: float32 [16, 1024, 1024], P('exp', 'dp')
- new_in_mean: float32 [16, 1024, 1024], P('exp', 'dp')
- new_in_square: float32 [16, 1024, 1024], P('exp', 'dp')
- new_down: float32 [16, 1024, 512], P('exp', 'dp')
- new_down_mean: float32 [16, 1024, 512], P('exp', 'dp')
- new_down_square: float32 [16, 1024, 512], P('exp', 'dp')
Inputs may be any that keep to these rules, and one draw needn't show every extreme that they name: `doc_lengths`: row b lists the lengths of the 3 documents of block b in order; they sum to 64, and the longest is exactly 48. `routes`: each row names 8 different experts. In each aligned block of 64 rows (one micro-batch of one device) no expert is named by more than 40 rows, a bound that some block reaches.
All inputs are finite; a program needn't handle non-finite values.
Results may differ from a plain program's by a relative error of at most 0.02.
Values may be sent and summed in bfloat16 or wider, within the bound.
No kernel may reach another device: no remote copies, remote signals or barrier semaphores. Data moves between devices by JAX's collectives and lax.ppermute only.
A program may use at most 192 MiB of HBM per device.

v0:
```python
import math

import jax
import jax.numpy as jnp
from jax import lax
from jax.sharding import PartitionSpec as P

QUERY_HEADS = 16
KEY_VALUE_HEADS = 8
HEAD_DIMENSION = 64
FF = 512
STEP = 10
CAP = 40


norm_eps = 1e-06
rope_base = 10000.0
mask_fill = -1e30
beta_one = 0.9
beta_two = 0.95
adam_eps = 1e-08
decay_rate = 0.1


def rms_scale(values):
    return lax.rsqrt(jnp.mean(values * values, axis=-1, keepdims=True) + norm_eps)


def doc_layout(doc_lens, sequence_length):
    row_index = jnp.arange(sequence_length, dtype=jnp.int32)
    doc_ends = jnp.cumsum(doc_lens, dtype=jnp.int32)
    passed = (row_index[:, None] >= doc_ends[None, :]).astype(jnp.int32)
    segment = jnp.sum(passed, axis=1, dtype=jnp.int32)
    starts = jnp.sum(passed * doc_lens[None, :], axis=1, dtype=jnp.int32)
    return ((row_index - starts).astype(jnp.float32), segment)


def rope_tables(positions, head_size):
    half_size = head_size // 2
    freq_index = jnp.arange(half_size, dtype=jnp.float32)
    inverse = jnp.exp(freq_index * (-2.0 * math.log(rope_base) / head_size))
    angles = positions[:, None] * inverse[None, :]
    return (jnp.cos(angles)[:, None, :], jnp.sin(angles)[:, None, :])


def rotary_apply(values, cosine_table, sine_table):
    half_size = values.shape[-1] // 2
    lower_half = values[..., :half_size]
    upper_half = values[..., half_size:]
    return jnp.concatenate(
        [
            lower_half * cosine_table - upper_half * sine_table,
            upper_half * cosine_table + lower_half * sine_table,
        ],
        axis=-1,
    )


def rotate_back(values, cosine_table, sine_table):
    half_size = values.shape[-1] // 2
    lower_half = values[..., :half_size]
    upper_half = values[..., half_size:]
    return jnp.concatenate(
        [
            lower_half * cosine_table + upper_half * sine_table,
            upper_half * cosine_table - lower_half * sine_table,
        ],
        axis=-1,
    )


def adamw(weight, gradient, mean_old, square_old, step_rate, weight_decay):
    mean_new = beta_one * mean_old + (1.0 - beta_one) * gradient
    square_new = beta_two * square_old + (1.0 - beta_two) * gradient * gradient
    corrected = (
        mean_new
        / (1.0 - beta_one**STEP)
        / (jnp.sqrt(square_new / (1.0 - beta_two**STEP)) + adam_eps)
    )
    return (weight - step_rate * (corrected + weight_decay * weight), mean_new, square_new)


def dense_products(factor_lists):
    normed = jnp.concatenate([member[0] for member in factor_lists], axis=0)
    projected_grad = jnp.concatenate([member[1] for member in factor_lists], axis=0)
    attended = jnp.concatenate([member[2] for member in factor_lists], axis=0)
    branch_grad = jnp.concatenate([member[3] for member in factor_lists], axis=0)
    normed_two = jnp.concatenate([member[4] for member in factor_lists], axis=0)
    logit_grad = jnp.concatenate([member[5] for member in factor_lists], axis=0)
    gains_grad = factor_lists[0][6]
    for member in factor_lists[1:]:
        gains_grad = gains_grad + member[6]
    qkv_grad = jnp.einsum("td,tf->df", normed, projected_grad, preferred_element_type=jnp.float32)
    out_grad = jnp.einsum("td,th->dh", branch_grad, attended, preferred_element_type=jnp.float32)
    router_grad = jnp.einsum(
        "td,te->de", normed_two, logit_grad, preferred_element_type=jnp.float32
    )
    return (qkv_grad, out_grad, router_grad, gains_grad)


def expert_products(factor_lists):
    kept_rows = jnp.concatenate([member[0] for member in factor_lists], axis=2)
    inner_grad = jnp.concatenate([member[1] for member in factor_lists], axis=2)
    grad_arrived = jnp.concatenate([member[2] for member in factor_lists], axis=2)
    activation = jnp.concatenate([member[3] for member in factor_lists], axis=2)
    in_grad = jnp.einsum(
        "aecd,aecf->edf", kept_rows, inner_grad, preferred_element_type=jnp.float32
    )
    down_grad = jnp.einsum(
        "aecd,aecf->edf", grad_arrived, activation, preferred_element_type=jnp.float32
    )
    return (in_grad, down_grad)


def micro_step(block_tokens, block_cot, block_lens, block_routes, weights):
    qkv_full, out_full, router_full, gain_pair, in_full, down_full = weights
    sequence_length, model_width = block_tokens.shape
    top_count = block_routes.shape[1]
    experts_all = router_full.shape[1]
    local_experts = in_full.shape[0]
    group_count = lax.axis_size("exp")
    pair_count = sequence_length * top_count
    slot_count = experts_all * CAP
    head_group_size = QUERY_HEADS // KEY_VALUE_HEADS
    query_total_width = QUERY_HEADS * HEAD_DIMENSION
    key_value_width = KEY_VALUE_HEADS * HEAD_DIMENSION
    score_scale = HEAD_DIMENSION ** (-0.5)
    first_gain = gain_pair[:, 0]
    second_gain = gain_pair[:, 1]
    residual = block_tokens.astype(jnp.float32)
    positions, segment = doc_layout(block_lens, sequence_length)
    cosine_table, sine_table = rope_tables(positions, HEAD_DIMENSION)
    row_index = jnp.arange(sequence_length, dtype=jnp.int32)
    allowed = (segment[:, None] == segment[None, :]) & (row_index[None, :] <= row_index[:, None])
    first_scale = rms_scale(residual)
    normed = (residual * first_scale * first_gain).astype(jnp.bfloat16)
    projected_output = jnp.dot(normed, qkv_full, preferred_element_type=jnp.float32)
    query_rows = (
        rotary_apply(
            projected_output[:, :query_total_width].reshape(
                sequence_length, QUERY_HEADS, HEAD_DIMENSION
            ),
            cosine_table,
            sine_table,
        )
        .astype(jnp.bfloat16)
        .reshape(sequence_length, KEY_VALUE_HEADS, head_group_size, HEAD_DIMENSION)
    )
    key_matrix_rows = rotary_apply(
        projected_output[:, query_total_width : query_total_width + key_value_width].reshape(
            sequence_length, KEY_VALUE_HEADS, HEAD_DIMENSION
        ),
        cosine_table,
        sine_table,
    ).astype(jnp.bfloat16)
    value_matrix_rows = (
        projected_output[:, query_total_width + key_value_width :]
        .reshape(sequence_length, KEY_VALUE_HEADS, HEAD_DIMENSION)
        .astype(jnp.bfloat16)
    )

    def score_block():
        raw_scores = (
            jnp.einsum(
                "tkgd,skd->kgts", query_rows, key_matrix_rows, preferred_element_type=jnp.float32
            )
            * score_scale
        )
        return jnp.where(allowed, raw_scores, mask_fill)

    scores = score_block()
    row_peak = jnp.max(scores, axis=-1, keepdims=True)
    log_total = row_peak + jnp.log(jnp.sum(jnp.exp(scores - row_peak), axis=-1, keepdims=True))
    attention_weights = jnp.exp(scores - log_total).astype(jnp.bfloat16)
    attended = jnp.einsum(
        "kgts,skd->tkgd", attention_weights, value_matrix_rows, preferred_element_type=jnp.float32
    )
    attended = attended.reshape(sequence_length, query_total_width).astype(jnp.bfloat16)
    branch = jnp.einsum("th,dh->td", attended, out_full, preferred_element_type=jnp.float32)
    hidden = residual + branch
    second_scale = rms_scale(hidden)
    normed_two = (hidden * second_scale * second_gain).astype(jnp.bfloat16)
    logits = jnp.dot(normed_two, router_full, preferred_element_type=jnp.float32)
    picked = (
        block_routes[:, :, None] == jnp.arange(experts_all, dtype=jnp.int32)[None, None, :]
    ).astype(jnp.float32)
    gates = jax.nn.softmax(jnp.sum(picked * logits[:, None, :], axis=-1), axis=-1)
    flat_routes = block_routes.reshape(pair_count)
    expert_hits = (
        flat_routes[:, None] == jnp.arange(experts_all, dtype=jnp.int32)[None, :]
    ).astype(jnp.int32)
    earlier_hits = jnp.cumsum(expert_hits, axis=0, dtype=jnp.int32) - expert_hits
    slot_of_pair = flat_routes * CAP + jnp.sum(earlier_hits * expert_hits, axis=1, dtype=jnp.int32)
    slot_match = slot_of_pair[None, :] == jnp.arange(slot_count, dtype=jnp.int32)[:, None]
    pair_of_slot = jnp.sum(
        jnp.where(slot_match, jnp.arange(pair_count, dtype=jnp.int32)[None, :], 0),
        axis=1,
        dtype=jnp.int32,
    )
    slot_used = jnp.any(slot_match, axis=1)
    token_of_slot = pair_of_slot // top_count
    send_rows = jnp.where(
        slot_used[:, None], normed_two[token_of_slot], jnp.zeros((), jnp.bfloat16)
    )
    send_rows = send_rows.reshape(experts_all, CAP, model_width)
    arrived = lax.all_to_all(send_rows, "exp", split_axis=0, concat_axis=0, tiled=True)
    slot_width = arrived.shape[1]
    grouped_rows = arrived.reshape(group_count, local_experts, slot_width, model_width)
    inner_sums = jnp.einsum(
        "aecd,edf->aecf", grouped_rows, in_full, preferred_element_type=jnp.float32
    )
    activation = (jax.nn.silu(inner_sums[..., :FF]) * inner_sums[..., FF:]).astype(jnp.bfloat16)
    results = jnp.einsum(
        "aecf,edf->aecd", activation, down_full, preferred_element_type=jnp.float32
    ).astype(jnp.bfloat16)
    results = results.reshape(group_count * local_experts, slot_width, model_width)
    sent_back = lax.all_to_all(results, "exp", split_axis=0, concat_axis=0, tiled=True)
    inner_all = inner_sums.reshape(group_count * local_experts, slot_width, 2 * FF)
    pair_out = (
        sent_back.reshape(slot_count, model_width)[slot_of_pair]
        .astype(jnp.float32)
        .reshape(sequence_length, top_count, model_width)
    )
    block_out = (hidden + jnp.sum(gates[:, :, None] * pair_out, axis=1)).astype(jnp.bfloat16)
    upstream = block_cot.astype(jnp.float32)
    gate_grad = jnp.sum(upstream[:, None, :] * pair_out, axis=-1)
    pair_grad = (
        (gates[:, :, None] * upstream[:, None, :])
        .astype(jnp.bfloat16)
        .reshape(pair_count, model_width)
    )
    chosen_grad = gates * (gate_grad - jnp.sum(gates * gate_grad, axis=-1, keepdims=True))
    logit_grad = jnp.sum(picked * chosen_grad[:, :, None], axis=1).astype(jnp.bfloat16)
    normed_two_grad = jnp.einsum(
        "te,de->td", logit_grad, router_full, preferred_element_type=jnp.float32
    )
    grad_rows = jnp.where(slot_used[:, None], pair_grad[pair_of_slot], jnp.zeros((), jnp.bfloat16))
    grad_rows = grad_rows.reshape(experts_all, CAP, model_width)
    grad_arrived = lax.all_to_all(grad_rows, "exp", split_axis=0, concat_axis=0, tiled=True)
    grad_arrived = grad_arrived.reshape(group_count, local_experts, CAP, model_width)
    kept_rows = arrived.reshape(group_count, local_experts, CAP, model_width)
    kept_inner = inner_all.reshape(group_count, local_experts, CAP, 2 * FF)
    gate_part = kept_inner[..., :FF]
    up_part = kept_inner[..., FF:]
    gate_sigmoid = jax.nn.sigmoid(gate_part)
    gate_silu = jax.nn.silu(gate_part)
    activation = (gate_silu * up_part).astype(jnp.bfloat16)
    activation_grad = jnp.einsum(
        "aecd,edf->aecf", grad_arrived, down_full, preferred_element_type=jnp.float32
    )
    inner_grad = jnp.concatenate(
        [
            activation_grad * up_part * gate_sigmoid * (1.0 + gate_part * (1.0 - gate_sigmoid)),
            activation_grad * gate_silu,
        ],
        axis=-1,
    ).astype(jnp.bfloat16)
    copy_grads = jnp.einsum(
        "aecf,edf->aecd", inner_grad, in_full, preferred_element_type=jnp.float32
    ).astype(jnp.bfloat16)
    copy_grads = copy_grads.reshape(group_count * local_experts, CAP, model_width)
    copy_back = lax.all_to_all(copy_grads, "exp", split_axis=0, concat_axis=0, tiled=True).reshape(
        slot_count, model_width
    )
    per_pair = (
        copy_back[slot_of_pair].astype(jnp.float32).reshape(sequence_length, top_count, model_width)
    )
    normed_two_grad = normed_two_grad + jnp.sum(per_pair, axis=1)
    scaled_two = normed_two_grad * second_gain
    second_gain_grad = jnp.sum(normed_two_grad * hidden * second_scale, axis=0)
    hidden_grad = (
        upstream
        + second_scale * scaled_two
        - hidden * second_scale**3 * jnp.mean(scaled_two * hidden, axis=-1, keepdims=True)
    )
    branch_grad = hidden_grad.astype(jnp.bfloat16)
    attended_output_grad = jnp.einsum(
        "td,dh->th", branch_grad, out_full, preferred_element_type=jnp.float32
    )
    attended_output_grad = attended_output_grad.astype(jnp.bfloat16).reshape(
        sequence_length, KEY_VALUE_HEADS, head_group_size, HEAD_DIMENSION
    )
    scores_again = score_block()
    attention_again = jnp.exp(scores_again - log_total)
    value_grad = jnp.einsum(
        "kgts,tkgd->skd",
        attention_again.astype(jnp.bfloat16),
        attended_output_grad,
        preferred_element_type=jnp.float32,
    )
    weight_grad = jnp.einsum(
        "tkgd,skd->kgts",
        attended_output_grad,
        value_matrix_rows,
        preferred_element_type=jnp.float32,
    )
    row_delta = jnp.sum(attention_again * weight_grad, axis=-1, keepdims=True)
    score_grad = (attention_again * (weight_grad - row_delta)).astype(jnp.bfloat16)
    query_grad = (
        jnp.einsum(
            "kgts,skd->tkgd", score_grad, key_matrix_rows, preferred_element_type=jnp.float32
        )
        * score_scale
    )
    key_grad = (
        jnp.einsum("kgts,tkgd->skd", score_grad, query_rows, preferred_element_type=jnp.float32)
        * score_scale
    )
    query_grad = rotate_back(
        query_grad.reshape(sequence_length, QUERY_HEADS, HEAD_DIMENSION), cosine_table, sine_table
    ).reshape(sequence_length, query_total_width)
    key_grad = rotate_back(key_grad, cosine_table, sine_table).reshape(
        sequence_length, key_value_width
    )
    projected_grad = jnp.concatenate(
        [query_grad, key_grad, value_grad.reshape(sequence_length, key_value_width)], axis=-1
    ).astype(jnp.bfloat16)
    normed_grad = jnp.einsum(
        "tf,df->td", projected_grad, qkv_full, preferred_element_type=jnp.float32
    )
    scaled_one = normed_grad * first_gain
    first_gain_grad = jnp.sum(normed_grad * residual * first_scale, axis=0)
    input_grad = (
        hidden_grad
        + first_scale * scaled_one
        - residual * first_scale**3 * jnp.mean(scaled_one * residual, axis=-1, keepdims=True)
    ).astype(jnp.bfloat16)
    gains_grad = jnp.stack([first_gain_grad, second_gain_grad], axis=1)
    dense_factors = (
        normed,
        projected_grad,
        attended,
        branch_grad,
        normed_two,
        logit_grad,
        gains_grad,
    )
    expert_factors = (kept_rows, inner_grad, grad_arrived, activation)
    return (block_out, input_grad, dense_factors, expert_factors)


def body(
    tokens,
    cotangent,
    doc_lengths,
    routes,
    qkv_weight,
    qkv_mean,
    qkv_square,
    out_weight,
    out_mean,
    out_square,
    router_weight,
    router_mean,
    router_square,
    norm_gains,
    gains_mean,
    gains_square,
    in_weight,
    in_mean,
    in_square,
    down_weight,
    down_mean,
    down_square,
):
    qkv_full, out_full, router_full, gains_full = (
        lax.all_gather(qkv_weight.astype(jnp.bfloat16), ("dp", "exp"), axis=0, tiled=True),
        lax.all_gather(out_weight.astype(jnp.bfloat16), ("dp", "exp"), axis=0, tiled=True),
        lax.all_gather(router_weight.astype(jnp.bfloat16), ("dp", "exp"), axis=0, tiled=True),
        lax.all_gather(norm_gains.astype(jnp.bfloat16), ("dp", "exp"), axis=0, tiled=True),
    )
    in_full, down_full = (
        lax.all_gather(in_weight.astype(jnp.bfloat16), "dp", axis=1, tiled=True),
        lax.all_gather(down_weight.astype(jnp.bfloat16), "dp", axis=1, tiled=True),
    )
    weights = (qkv_full, out_full, router_full, gains_full.astype(jnp.float32), in_full, down_full)
    micro_count = doc_lengths.shape[0]
    block_rows = tokens.shape[0] // micro_count
    produced_list = []
    grad_list = []
    dense_total = None
    expert_total = None
    dense_factor_list = []
    expert_factor_list = []
    for batch_index in range(micro_count):
        row_start = batch_index * block_rows
        produced, token_grad, dense_factors, expert_factors = micro_step(
            tokens[row_start : row_start + block_rows],
            cotangent[row_start : row_start + block_rows],
            doc_lengths[batch_index],
            routes[row_start : row_start + block_rows],
            weights,
        )
        dense_factor_list.append(dense_factors)
        expert_factor_list.append(expert_factors)
        produced_list.append(produced)
        grad_list.append(token_grad)
    qkv_grad, out_grad, router_grad, gains_grad = dense_products(dense_factor_list)
    in_grad, down_grad = expert_products(expert_factor_list)
    dense_total = (
        lax.psum_scatter(qkv_grad, ("dp", "exp"), scatter_dimension=0, tiled=True),
        lax.psum_scatter(out_grad, ("dp", "exp"), scatter_dimension=0, tiled=True),
        lax.psum_scatter(router_grad, ("dp", "exp"), scatter_dimension=0, tiled=True),
        lax.psum_scatter(gains_grad, ("dp", "exp"), scatter_dimension=0, tiled=True),
    )
    expert_total = (
        lax.psum_scatter(
            in_grad.astype(jnp.bfloat16), "dp", scatter_dimension=1, tiled=True
        ).astype(jnp.float32),
        lax.psum_scatter(
            down_grad.astype(jnp.bfloat16), "dp", scatter_dimension=1, tiled=True
        ).astype(jnp.float32),
    )
    d_qkv, d_out, d_router, d_gains = dense_total
    d_in, d_down = expert_total
    block_out = jnp.concatenate(produced_list, axis=0)
    input_grad = jnp.concatenate(grad_list, axis=0)
    new_qkv, new_qkv_mean, new_qkv_square = adamw(
        qkv_weight, d_qkv, qkv_mean, qkv_square, 0.15, decay_rate
    )
    new_out, new_out_mean, new_out_square = adamw(
        out_weight, d_out, out_mean, out_square, 0.3, decay_rate
    )
    new_router, new_router_mean, new_router_square = adamw(
        router_weight, d_router, router_mean, router_square, 0.05, decay_rate
    )
    new_gains, new_gains_mean, new_gains_square = adamw(
        norm_gains, d_gains, gains_mean, gains_square, 0.8, 0.0
    )
    new_in, new_in_mean, new_in_square = adamw(in_weight, d_in, in_mean, in_square, 0.1, decay_rate)
    new_down, new_down_mean, new_down_square = adamw(
        down_weight, d_down, down_mean, down_square, 1.0, decay_rate
    )
    return (
        block_out,
        input_grad,
        new_qkv,
        new_qkv_mean,
        new_qkv_square,
        new_out,
        new_out_mean,
        new_out_square,
        new_router,
        new_router_mean,
        new_router_square,
        new_gains,
        new_gains_mean,
        new_gains_square,
        new_in,
        new_in_mean,
        new_in_square,
        new_down,
        new_down_mean,
        new_down_square,
    )


def solution(mesh):
    placed = (
        P(("dp", "exp"), None),
        P(("dp", "exp"), None),
        P(("dp", "exp"), None),
        P(("dp", "exp"), None),
        P(("dp", "exp"), None),
        P(("dp", "exp"), None),
        P(("dp", "exp"), None),
        P(("dp", "exp"), None),
        P(("dp", "exp"), None),
        P(("dp", "exp"), None),
        P(("dp", "exp"), None),
        P(("dp", "exp"), None),
        P(("dp", "exp"), None),
        P(("dp", "exp"), None),
        P(("dp", "exp"), None),
        P(("dp", "exp"), None),
        P("exp", "dp", None),
        P("exp", "dp", None),
        P("exp", "dp", None),
        P("exp", "dp", None),
        P("exp", "dp", None),
        P("exp", "dp", None),
    )
    return jax.shard_map(
        body,
        mesh=mesh,
        in_specs=placed,
        out_specs=(
            P(("dp", "exp"), None),
            P(("dp", "exp"), None),
            P(("dp", "exp"), None),
            P(("dp", "exp"), None),
            P(("dp", "exp"), None),
            P(("dp", "exp"), None),
            P(("dp", "exp"), None),
            P(("dp", "exp"), None),
            P(("dp", "exp"), None),
            P(("dp", "exp"), None),
            P(("dp", "exp"), None),
            P(("dp", "exp"), None),
            P(("dp", "exp"), None),
            P(("dp", "exp"), None),
            P("exp", "dp", None),
            P("exp", "dp", None),
            P("exp", "dp", None),
            P("exp", "dp", None),
            P("exp", "dp", None),
            P("exp", "dp", None),
        ),
        check_vma=False,
    )
```

profile of v0, /device:TPU:0, one launch (start us, length us, event | category | flops | bytes accessed | tf_op | source)
XLA Modules:
  0.0 1422.9 jit_solution(16625325738890553936)
XLA Ops:
  16.0 69.3 %all-gather = bf16[32,32,2]{1,2,0:T(2,128)(2,1)S(1)} all-gather(bf16[1,32,2]{1,2,0:T(2,128)(2,1)S(1)} %convert_bitcast_fusion.1), channel_id=1, replica_groups=mesh['dp'=16,'exp'=2] {'dp','exp'}, dimensions={0}, use_global_device_ids=true | all-gather | bytes 4224 | tf_op jit(solution)/shard_map/all_gather | solution.py:370
  90.5 64.6 %all-gather.1 = bf16[32,32,16]{1,2,0:T(8,128)(2,1)S(1)} all-gather(bf16[1,32,16]{1,2,0:T(8,128)(2,1)S(1)} %convert_bitcast_fusion), channel_id=1, replica_groups=mesh['dp'=16,'exp'=2] {'dp','exp'}, dimensions={0}, use_global_device_ids=true | all-gather | bytes 33792 | tf_op jit(solution)/shard_map/all_gather | solution.py:369
  191.8 9.7 all-to-all-done
  201.5 4.8 all-to-all-start.4
  206.3 57.6 %all-gather.11.cloned.1.call-done = bf16[8,1024,1024]{2,1,0:T(8,128)(2,1)} async-done(((bf16[8,64,1024]{2,1,0:T(8,128)(2,1)}), bf16[8,1024,1024]{2,1,0:T(8,128)(2,1)}) %all-gather.11.cloned.1.call-update) | async-done | bytes 16777232 | tf_op jit(solution)/shard_map/all_gather | solution.py:373
  263.9 10.3 fusion.33
  274.2 65.5 %all-gather.13.cloned.1.call-done = bf16[8,1024,512]{2,1,0:T(8,128)(2,1)} async-done(((bf16[8,64,512]{2,1,0:T(8,128)(2,1)}), bf16[8,1024,512]{2,1,0:T(8,128)(2,1)}) %all-gather.13.cloned.1.call-update) | async-done | bytes 8388624 | tf_op jit(solution)/shard_map/all_gather | solution.py:374
  339.7 7.4 multiply_convert_fusion.3
  347.1 11.4 fusion.60
  364.3 6.2 fusion.54
  371.7 8.7 all-to-all-done.5
  380.4 4.2 all-to-all-start.1
  393.0 7.9 all-to-all-done.1
  422.9 14.6 %all-to-all-done.2 = bf16[16,40,1024]{2,1,0:T(8,128)(2,1)S(1)} async-done(((bf16[16,40,1024]{2,1,0:T(8,128)(2,1)}), bf16[16,40,1024]{2,1,0:T(8,128)(2,1)S(1)}, u32[]{:S(2)}, u32[]{:S(2)}) %all-to-all-start.2) | async-done | bytes 1310752 | tf_op jit(solution)/shard_map/all_to_all | solution.py:206
  441.1 10.3 fusion.36
  451.4 4.2 all-to-all-done.6
  456.6 7.4 multiply_convert_fusion.1
  464.0 6.3 fusion.51
  471.4 3.8 all-to-all-start.3
  475.2 11.4 fusion.57
  498.2 6.8 all-to-all-done.7
  537.3 6.1 bitcast_convert_fusion.1
  544.5 4.5 fusion.98
  550.8 10.0 bitcast_convert_fusion
  563.5 99.5 %reduce-scatter.21.cloned.1.call-done = f32[32,2]{1,0:T(8,128)} async-done(((f32[1024,2]{1,0:T(8,128)}), f32[32,2]{1,0:T(8,128)}) %reduce-scatter.21.cloned.1.call-update) | async-done | bytes 272
  664.3 131.3 %reduce-scatter.19.cloned.1.call-done = f32[32,16]{1,0:T(8,128)} async-done(((f32[1024,16]{1,0:T(8,128)}), f32[32,16]{1,0:T(8,128)}) %reduce-scatter.19.cloned.1.call-update) | async-done | bytes 2064
  797.1 138.2 %reduce-scatter.13.cloned.1.call-done = f32[32,1024]{1,0:T(8,128)} async-done(((f32[1024,1024]{1,0:T(8,128)}), f32[32,1024]{1,0:T(8,128)}) %reduce-scatter.13.cloned.1.call-update) | async-done | bytes 131088 | tf_op jit(solution)/shard_map/reduce_scatter | solution.py:402
  936.9 104.1 %reduce-scatter.17.cloned.1.call-done = bf16[8,64,512]{2,1,0:T(8,128)(2,1)} async-done(((bf16[8,1024,512]{2,1,0:T(8,128)(2,1)}), bf16[8,64,512]{2,1,0:T(8,128)(2,1)}) %reduce-scatter.17.cloned.1.call-update) | async-done | bytes 524304 | tf_op jit(solution)/shard_map/reduce_scatter | solution.py:410
  1041.1 4.1 add_subtract_fusion
  1045.1 181.1 %reduce-scatter.11.cloned.1.call-done = f32[32,2048]{1,0:T(8,128)} async-done(((f32[1024,2048]{1,0:T(8,128)}), f32[32,2048]{1,0:T(8,128)}) %reduce-scatter.11.cloned.1.call-update) | async-done | bytes 262160 | tf_op jit(solution)/shard_map/reduce_scatter | solution.py:401
  1228.3 180.8 %reduce-scatter.15.cloned.1.call-done = bf16[8,64,1024]{2,1,0:T(8,128)(2,1)} async-done(((bf16[8,1024,1024]{2,1,0:T(8,128)(2,1)}), bf16[8,64,1024]{2,1,0:T(8,128)(2,1)}) %reduce-scatter.15.cloned.1.call-update) | async-done | bytes 1048592 | tf_op jit(solution)/shard_map/reduce_scatter | solution.py:407
  1409.2 6.5 multiply_subtract_fusion
  (536 shorter events, 147.6 us)
Async XLA Ops:
  7.2 152.8 %all-gather.7.cloned.1.call-start = ((), (), s32[]{:S(2)}) async-start(), calls=%async_computation.14 | async-start | bytes 4325376 | tf_op jit(solution)/shard_map/all_gather | solution.py:367
  8.9 159.9 %all-gather.9.cloned.1.call-start = ((), (), s32[]{:S(2)}) async-start(), calls=%async_computation.15 | async-start | bytes 2162688 | tf_op jit(solution)/shard_map/all_gather | solution.py:368
  10.5 253.4 %all-gather.11.cloned.1.call-start = ((), (), s32[]{:S(2)}) async-start(), calls=%async_computation.16 | async-start | bytes 17825792 | tf_op jit(solution)/shard_map/all_gather | solution.py:373
  13.4 144.4 %copy-start.6 = (bf16[128,1024]{1,0:T(8,128)(2,1)S(1)}, bf16[128,1024]{1,0:T(8,128)(2,1)}, u32[]{:S(2)}) copy-start(bf16[128,1024]{1,0:T(8,128)(2,1)} %param.22) | copy-start | bytes 786436
  13.4 145.7 %copy-start.63 = (bf16[128,1024]{1,0:T(8,128)(2,1)S(1)}, bf16[128,1024]{1,0:T(8,128)(2,1)}, u32[]{:S(2)}) copy-start(bf16[128,1024]{1,0:T(8,128)(2,1)} %param.23) | copy-start | bytes 786436
  13.4 326.2 %all-gather.13.cloned.1.call-start = ((), (), s32[]{:S(2)}) async-start(), calls=%async_computation.17 | async-start | bytes 8912896 | tf_op jit(solution)/shard_map/all_gather | solution.py:374
  15.1 157.6 %copy-start.103 = (s32[64,8]{0,1:T(8,128)}, s32[64,8]{0,1:T(8,128)S(1)}, u32[]{:S(2)}) copy-start(s32[64,8]{0,1:T(8,128)S(1)} %get-tuple-element.112) | copy-start | bytes 6148
  183.7 17.8 %all-to-all-start = ((bf16[16,40,1024]{2,1,0:T(8,128)(2,1)}), bf16[16,40,1024]{2,1,0:T(8,128)(2,1)S(1)}, u32[]{:S(2)}, u32[]{:S(2)}) async-start(bf16[16,40,1024]{2,1,0:T(8,128)(2,1)} %get-tuple-element.114), calls=%async_computation | async-start | bytes 2621440 | tf_op jit(solution)/shard_map/all_to_all | solution.py:206
  189.9 173.4 %copy-start.53 = (bf16[64,8,64]{2,1,0:T(8,128)(2,1)}, bf16[64,8,64]{2,1,0:T(8,128)(2,1)S(1)}, u32[]{:S(2)}) copy-start(bf16[64,8,64]{2,1,0:T(8,128)(2,1)S(1)} %convert_element_type.276) | copy-start | bytes 196612
  191.6 171.7 %copy-start.3 = (f32[8,2,64,64]{2,3,1,0:T(8,128)}, f32[8,2,64,64]{2,3,1,0:T(8,128)S(1)}, u32[]{:S(2)}) copy-start(f32[8,2,64,64]{2,3,1,0:T(8,128)S(1)} %get-tuple-element.140) | copy-start | bytes 786436
  201.5 72.7 %all-to-all-start.4 = ((bf16[16,40,1024]{2,1,0:T(8,128)(2,1)}), bf16[16,40,1024]{2,1,0:T(8,128)(2,1)}, u32[]{:S(2)}, u32[]{:S(2)}) async-start(bf16[16,40,1024]{2,1,0:T(8,128)(2,1)} %get-tuple-element.113), calls=%async_computation.4 | async-start | bytes 2621440 | tf_op jit(solution)/shard_map/all_to_all | solution.py:239
  359.7 20.7 %all-to-all-start.5 = ((bf16[16,40,1024]{2,1,0:T(8,128)(2,1)}), bf16[16,40,1024]{2,1,0:T(8,128)(2,1)S(1)}, u32[]{:S(2)}, u32[]{:S(2)}) async-start(bf16[16,40,1024]{2,1,0:T(8,128)(2,1)} %bitcast.314), calls=%async_computation.5 | async-start | bytes 2621440 | tf_op jit(solution)/shard_map/all_to_all | solution.py:262
  380.4 20.5 %all-to-all-start.1 = ((bf16[16,40,1024]{2,1,0:T(8,128)(2,1)}), bf16[16,40,1024]{2,1,0:T(8,128)(2,1)S(1)}, u32[]{:S(2)}, u32[]{:S(2)}) async-start(bf16[16,40,1024]{2,1,0:T(8,128)(2,1)} %bitcast.313), calls=%async_computation.1 | async-start | bytes 2621440 | tf_op jit(solution)/shard_map/all_to_all | solution.py:217
  418.4 19.1 %all-to-all-start.2 = ((bf16[16,40,1024]{2,1,0:T(8,128)(2,1)}), bf16[16,40,1024]{2,1,0:T(8,128)(2,1)S(1)}, u32[]{:S(2)}, u32[]{:S(2)}) async-start(bf16[16,40,1024]{2,1,0:T(8,128)(2,1)} %get-tuple-element.116), calls=%async_computation.2 | async-start | bytes 2621440 | tf_op jit(solution)/shard_map/all_to_all | solution.py:206
  437.5 18.1 %all-to-all-start.6 = ((bf16[16,40,1024]{2,1,0:T(8,128)(2,1)}), bf16[16,40,1024]{2,1,0:T(8,128)(2,1)S(1)}, u32[]{:S(2)}, u32[]{:S(2)}) async-start(bf16[16,40,1024]{2,1,0:T(8,128)(2,1)} %get-tuple-element.115), calls=%async_computation.6 | async-start | bytes 2621440 | tf_op jit(solution)/shard_map/all_to_all | solution.py:239
  471.4 17.3 %all-to-all-start.3 = ((bf16[16,40,1024]{2,1,0:T(8,128)(2,1)}), bf16[16,40,1024]{2,1,0:T(8,128)(2,1)S(1)}, u32[]{:S(2)}, u32[]{:S(2)}) async-start(bf16[16,40,1024]{2,1,0:T(8,128)(2,1)} %bitcast.315), calls=%async_computation.3 | async-start | bytes 2621440 | tf_op jit(solution)/shard_map/all_to_all | solution.py:217
  488.7 16.2 %all-to-all-start.7 = ((bf16[16,40,1024]{2,1,0:T(8,128)(2,1)}), bf16[16,40,1024]{2,1,0:T(8,128)(2,1)S(1)}, u32[]{:S(2)}, u32[]{:S(2)}) async-start(bf16[16,40,1024]{2,1,0:T(8,128)(2,1)} %bitcast.312), calls=%async_computation.7 | async-start | bytes 2621440 | tf_op jit(solution)/shard_map/all_to_all | solution.py:262
  492.4 170.5 %reduce-scatter.21.cloned.1.call-start = ((), (), s32[]{:S(2)}) async-start(), calls=%async_computation.23 | async-start | bytes 540672
  531.5 264.2 %reduce-scatter.19.cloned.1.call-start = ((), (), s32[]{:S(2)}) async-start(), calls=%async_computation.22 | async-start | bytes 540672
  532.7 402.6 %reduce-scatter.13.cloned.1.call-start = ((), (), s32[]{:S(2)}) async-start(), calls=%async_computation.19 | async-start | bytes 4325376 | tf_op jit(solution)/shard_map/reduce_scatter | solution.py:402
  535.7 505.4 %reduce-scatter.17.cloned.1.call-start = ((), (), s32[]{:S(2)}) async-start(), calls=%async_computation.21 | async-start | bytes 8912896 | tf_op jit(solution)/shard_map/reduce_scatter | solution.py:410
  543.5 682.7 %reduce-scatter.11.cloned.1.call-start = ((), (), s32[]{:S(2)}) async-start(), calls=%async_computation.18 | async-start | bytes 8650752 | tf_op jit(solution)/shard_map/reduce_scatter | solution.py:401
  549.1 860.0 %reduce-scatter.15.cloned.1.call-start = ((), (), s32[]{:S(2)}) async-start(), calls=%async_computation.20 | async-start | bytes 17825792 | tf_op jit(solution)/shard_map/reduce_scatter | solution.py:407
  560.9 235.5 %copy-start.112 = (f32[32,16]{0,1:T(8,128)S(1)}, f32[32,16]{0,1:T(8,128)}, u32[]{:S(2)}) copy-start(f32[32,16]{0,1:T(8,128)} %param.32) | copy-start | bytes 6148
  560.9 235.5 %copy-start.130 = (f32[32,16]{0,1:T(8,128)S(1)}, f32[32,16]{0,1:T(8,128)}, u32[]{:S(2)}) copy-start(f32[32,16]{0,1:T(8,128)} %param.33) | copy-start | bytes 6148
  560.9 235.5 %copy-start.131 = (f32[32,16]{0,1:T(8,128)S(1)}, f32[32,16]{0,1:T(8,128)}, u32[]{:S(2)}) copy-start(f32[32,16]{0,1:T(8,128)} %param.34) | copy-start | bytes 6148
  561.0 374.3 %copy-start.88 = (f32[32,1024]{1,0:T(8,128)S(1)}, f32[32,1024]{1,0:T(8,128)}, u32[]{:S(2)}) copy-start(f32[32,1024]{1,0:T(8,128)} %param.29) | copy-start | bytes 393220
  561.0 374.3 %copy-start.94 = (f32[32,1024]{1,0:T(8,128)S(1)}, f32[32,1024]{1,0:T(8,128)}, u32[]{:S(2)}) copy-start(f32[32,1024]{1,0:T(8,128)} %param.30) | copy-start | bytes 393220
  561.0 374.3 %copy-start.95 = (f32[32,1024]{1,0:T(8,128)S(1)}, f32[32,1024]{1,0:T(8,128)}, u32[]{:S(2)}) copy-start(f32[32,1024]{1,0:T(8,128)} %param.31) | copy-start | bytes 393220
  561.0 480.1 %copy-start.19 = (f32[8,64,512]{2,1,0:T(8,128)S(1)}, f32[8,64,512]{2,1,0:T(8,128)}, u32[]{:S(2)}) copy-start(f32[8,64,512]{2,1,0:T(8,128)} %param.41) | copy-start | bytes 3145732
  936.9 289.3 %copy-start.68 = (f32[32,2048]{1,0:T(8,128)S(1)}, f32[32,2048]{1,0:T(8,128)}, u32[]{:S(2)}) copy-start(f32[32,2048]{1,0:T(8,128)} %param.26) | copy-start | bytes 786436
  1041.1 368.1 %copy-start.5 = (f32[8,64,1024]{2,1,0:T(8,128)S(1)}, f32[8,64,1024]{2,1,0:T(8,128)}, u32[]{:S(2)}) copy-start(f32[8,64,1024]{2,1,0:T(8,128)} %param.38) | copy-start | bytes 6291460
  (139 other events, 1076.8 us)
Sparse Core Ops, SparseCore 0:
  11.5 64.7 all-gather.6
  80.0 55.4 all-gather.8
  138.2 125.7 all-gather.10
  266.6 73.0 all-gather.12
  531.6 131.2 reduce-scatter.20
  665.7 129.9 reduce-scatter.18
  797.9 137.2 reduce-scatter.12
  939.3 101.7 reduce-scatter.16
  1043.4 182.8 reduce-scatter.10
  1230.2 178.9 reduce-scatter.14
where the time goes:
time: 1430 us; the launch traced here: 1420 us
  waiting for transfers between devices  1010 us (71%)
  blocking collectives  134 us (9%)
  matrix products  124 us (9%)
  other arithmetic  53.5 us (4%)
  local copies, waits for them, and re-layouts  52.4 us (4%)
  starting transfers between devices  31.7 us (2%)
  between operations  16.8 us (1%)
    unnamed x12, waiting for transfers between devices  231 us
    reduce_scatter x1, waiting for transfers between devices, body(): lax.psum_scatter(qkv_grad, ('dp', 'exp'), scatter_dimension=0, tiled=True)  181 us
    reduce_scatter x1, waiting for transfers between devices, body(): lax.psum_scatter(in_grad.astype(jnp.bfloat16), 'dp', scatter_dimension=1,...  181 us
    reduce_scatter x1, waiting for transfers between devices, body(): lax.psum_scatter(out_grad, ('dp', 'exp'), scatter_dimension=0, tiled=True)  138 us
    reduce_scatter x1, waiting for transfers between devices, body(): lax.psum_scatter(down_grad.astype(jnp.bfloat16), 'dp', scatter_dimension=...  104 us
    all_gather x1, blocking collectives, body(): lax.all_gather(norm_gains.astype(jnp.bfloat16), ('dp', 'exp'), axis=0, ti...  69.3 us
    all_gather x1, waiting for transfers between devices, body(): lax.all_gather(down_weight.astype(jnp.bfloat16), 'dp', axis=1, tiled=True)  65.5 us
    all_gather x1, blocking collectives, body(): lax.all_gather(router_weight.astype(jnp.bfloat16), ('dp', 'exp'), axis=0,...  64.6 us
  transfers between devices with their start and end apart: 18, of which 15 were waited for; matrix products, arithmetic and copies ran while one was open for 9% of the time, Pallas kernels for 0%

commit v1 on v0

v1 whole, which is shorter than its diff:
```python
import math

import jax
import jax.numpy as jnp
import numpy as np
from jax import lax
from jax.sharding import Mesh
from jax.sharding import PartitionSpec as P

QUERY_HEADS = 16
KEY_VALUE_HEADS = 8
HEAD_DIMENSION = 64
FF = 512
STEP = 10
EXPERTS = 16
LANES = 128


norm_eps = 1e-06
rope_base = 10000.0
mask_fill = -1e30
beta_one = 0.9
beta_two = 0.95
adam_eps = 1e-08
decay_rate = 0.1


def rms_scale(values):
    return lax.rsqrt(jnp.mean(values * values, axis=-1, keepdims=True) + norm_eps)


def doc_layout(doc_lens, sequence_length):
    row_index = jnp.arange(sequence_length, dtype=jnp.int32)
    doc_ends = jnp.cumsum(doc_lens, dtype=jnp.int32)
    passed = (row_index[:, None] >= doc_ends[None, :]).astype(jnp.int32)
    segment = jnp.sum(passed, axis=1, dtype=jnp.int32)
    starts = jnp.sum(passed * doc_lens[None, :], axis=1, dtype=jnp.int32)
    return ((row_index - starts).astype(jnp.float32), segment)


def rope_tables(positions, head_size):
    half_size = head_size // 2
    freq_index = jnp.arange(half_size, dtype=jnp.float32)
    inverse = jnp.exp(freq_index * (-2.0 * math.log(rope_base) / head_size))
    angles = positions[:, None] * inverse[None, :]
    return (jnp.cos(angles)[:, None, :], jnp.sin(angles)[:, None, :])


def rotary_apply(values, cosine_table, sine_table):
    half_size = values.shape[-1] // 2
    lower_half = values[..., :half_size]
    upper_half = values[..., half_size:]
    return jnp.concatenate(
        [
            lower_half * cosine_table - upper_half * sine_table,
            upper_half * cosine_table + lower_half * sine_table,
        ],
        axis=-1,
    )


def rotate_back(values, cosine_table, sine_table):
    half_size = values.shape[-1] // 2
    lower_half = values[..., :half_size]
    upper_half = values[..., half_size:]
    return jnp.concatenate(
        [
            lower_half * cosine_table + upper_half * sine_table,
            upper_half * cosine_table - lower_half * sine_table,
        ],
        axis=-1,
    )


def adamw(weight, gradient, mean_old, square_old, step_rate, weight_decay):
    mean_new = beta_one * mean_old + (1.0 - beta_one) * gradient
    square_new = beta_two * square_old + (1.0 - beta_two) * gradient * gradient
    corrected = (
        mean_new
        / (1.0 - beta_one**STEP)
        / (jnp.sqrt(square_new / (1.0 - beta_two**STEP)) + adam_eps)
    )
    return (weight - step_rate * (corrected + weight_decay * weight), mean_new, square_new)


def order_of(kind, sizes):
    axes = {"home": (0, 1, 2, 3, 4), "dense": (2, 1, 3, 0, 4), "expert": (1, 2, 0, 3, 4)}[kind]
    return np.arange(math.prod(sizes), dtype=np.int32).reshape(sizes).transpose(axes).reshape(-1)


def reorder_matrix(before, after):
    return (jnp.asarray(before)[:, None] == jnp.asarray(after)[None, :]).astype(jnp.bfloat16)


def spread(values, axes):
    count = lax.axis_size(axes)
    copies = jnp.broadcast_to(values[None], (count,) + values.shape)
    return lax.all_to_all(copies, axes, split_axis=0, concat_axis=0, tiled=True)


def collect(values, axes):
    count = lax.axis_size(axes)
    parts = values.reshape((count, values.shape[0] // count) + values.shape[1:])
    parts = lax.all_to_all(parts, axes, split_axis=0, concat_axis=0, tiled=True)
    return jnp.sum(parts.astype(jnp.float32), axis=0)


def gather_dense(rows):
    width = rows.shape[1]
    rows = spread(rows, "a").reshape(-1, width)
    rows = spread(rows, ("r", "exp")).reshape(-1, width)
    return spread(rows, "core").reshape(-1, width)


def reduce_dense(grad):
    grad = collect(grad.astype(jnp.bfloat16), "core").astype(jnp.bfloat16)
    grad = collect(grad, ("r", "exp")).astype(jnp.bfloat16)
    return collect(grad, "a")


def body(
    tokens,
    cotangent,
    doc_lengths,
    routes,
    qkv_weight,
    qkv_mean,
    qkv_square,
    out_weight,
    out_mean,
    out_square,
    router_weight,
    router_mean,
    router_square,
    norm_gains,
    gains_mean,
    gains_square,
    in_weight,
    in_mean,
    in_square,
    down_weight,
    down_mean,
    down_square,
):
    f32, bf16 = jnp.float32, jnp.bfloat16
    n_a, n_r, n_c, n_e = (lax.axis_size(name) for name in ("a", "r", "core", "exp"))
    rows, width = tokens.shape
    experts = router_weight.shape[1]
    local_count = in_weight.shape[0]
    group_rows = n_c * n_a * rows
    sizes = (n_a, n_r, n_c, n_e, width // (n_a * n_r * n_c * n_e))
    home, dense, expert = (order_of(kind, sizes) for kind in ("home", "dense", "expert"))
    query_width = QUERY_HEADS * HEAD_DIMENSION
    key_width = KEY_VALUE_HEADS * HEAD_DIMENSION
    qkv_width = query_width + 2 * key_width
    fold = QUERY_HEADS // KEY_VALUE_HEADS
    score_scale = HEAD_DIMENSION ** (-0.5)

    local_rows = qkv_weight.shape[0]
    extra = jnp.zeros((local_rows, LANES - experts - 2), bf16)
    first_pack = jnp.concatenate(
        [qkv_weight.astype(bf16), router_weight.astype(bf16), norm_gains.astype(bf16), extra], axis=1
    )
    first_full = gather_dense(first_pack)
    out_full = gather_dense(out_weight.astype(bf16))
    to_dense = reorder_matrix(home, dense)
    cot_expert = jnp.dot(
        cotangent, reorder_matrix(home, expert), preferred_element_type=f32
    ).astype(bf16)
    cot_group = lax.all_gather(cot_expert, ("core", "a"), axis=0, tiled=True)
    expert_pack = jnp.concatenate([in_weight.astype(bf16), down_weight.astype(bf16)], axis=2)
    expert_pack = lax.all_to_all(expert_pack, ("core", "a"), split_axis=0, concat_axis=0, tiled=True)
    expert_full = lax.all_gather(expert_pack, ("exp", "r"), axis=0, tiled=True).reshape(
        n_e, width, 3 * FF
    )

    residual = jnp.dot(tokens, to_dense, preferred_element_type=f32)
    upstream = jnp.dot(cotangent, to_dense, preferred_element_type=f32)
    positions, segment = doc_layout(doc_lengths.reshape(-1), rows)
    cosine_table, sine_table = rope_tables(positions, HEAD_DIMENSION)
    row_index = jnp.arange(rows, dtype=jnp.int32)
    allowed = (segment[:, None] == segment[None, :]) & (row_index[None, :] <= row_index[:, None])
    qkv_full = first_full[:, :qkv_width]
    router_full = first_full[:, qkv_width : qkv_width + experts]
    gain_pair = first_full[:, qkv_width + experts : qkv_width + experts + 2].astype(f32)
    first_gain = gain_pair[:, 0]
    second_gain = gain_pair[:, 1]
    first_scale = rms_scale(residual)
    normed = (residual * first_scale * first_gain).astype(bf16)
    projected = jnp.dot(normed, qkv_full, preferred_element_type=f32)
    query_rows = (
        rotary_apply(
            projected[:, :query_width].reshape(rows, QUERY_HEADS, HEAD_DIMENSION),
            cosine_table,
            sine_table,
        )
        .astype(bf16)
        .reshape(rows, KEY_VALUE_HEADS, fold, HEAD_DIMENSION)
    )
    key_rows = rotary_apply(
        projected[:, query_width : query_width + key_width].reshape(
            rows, KEY_VALUE_HEADS, HEAD_DIMENSION
        ),
        cosine_table,
        sine_table,
    ).astype(bf16)
    value_rows = (
        projected[:, query_width + key_width :]
        .reshape(rows, KEY_VALUE_HEADS, HEAD_DIMENSION)
        .astype(bf16)
    )
    scores = (
        jnp.einsum("tkgd,skd->kgts", query_rows, key_rows, preferred_element_type=f32) * score_scale
    )
    scores = jnp.where(allowed, scores, mask_fill)
    row_peak = jnp.max(scores, axis=-1, keepdims=True)
    log_total = row_peak + jnp.log(jnp.sum(jnp.exp(scores - row_peak), axis=-1, keepdims=True))
    weights = jnp.exp(scores - log_total)
    attended = jnp.einsum(
        "kgts,skd->tkgd", weights.astype(bf16), value_rows, preferred_element_type=f32
    )
    attended = attended.reshape(rows, query_width).astype(bf16)
    hidden = residual + jnp.einsum("th,dh->td", attended, out_full, preferred_element_type=f32)
    second_scale = rms_scale(hidden)
    normed_two = (hidden * second_scale * second_gain).astype(bf16)
    logits = jnp.dot(normed_two, router_full, preferred_element_type=f32)
    expert_index = jnp.arange(experts, dtype=jnp.int32)
    used = jnp.any(routes[:, :, None] == expert_index[None, None, :], axis=1)
    gates = jax.nn.softmax(jnp.where(used, logits, -jnp.inf), axis=-1)
    gates_high = gates.astype(bf16)
    gates_low = (gates - gates_high.astype(f32)).astype(bf16)

    normed_expert = jnp.dot(
        normed_two, reorder_matrix(dense, expert), preferred_element_type=f32
    ).astype(bf16)
    sent = jnp.concatenate(
        [normed_expert, gates_high, gates_low, jnp.zeros((rows, LANES - 2 * experts), bf16)], axis=1
    )
    arrived = spread(sent, "a").reshape(n_a * rows, width + LANES)
    arrived = spread(arrived, "core").reshape(group_rows, width + LANES)
    group_normed = arrived[:, :width]
    group_gates = arrived[:, width:].astype(f32)
    place = lax.axis_index("core") * n_a + lax.axis_index("a")
    lane = jnp.arange(LANES, dtype=jnp.int32)
    cot_rows = cot_group.astype(f32)
    part_out = jnp.zeros((group_rows, width), f32)
    part_back = jnp.zeros((group_rows, width), f32)
    part_dots = jnp.zeros((group_rows, LANES), f32)
    expert_grads = []
    for index in range(n_e):
        number = index * local_count + place
        chosen = (lane % experts == number) & (lane < 2 * experts)
        gate = jnp.sum(jnp.where(chosen[None, :], group_gates, 0.0), axis=1, keepdims=True)
        in_full = expert_full[index, :, : 2 * FF]
        down_full = expert_full[index, :, 2 * FF :]
        inner = jnp.dot(group_normed, in_full, preferred_element_type=f32)
        gate_part = inner[:, :FF]
        up_part = inner[:, FF:]
        gate_sigmoid = jax.nn.sigmoid(gate_part)
        gate_silu = gate_part * gate_sigmoid
        activation = (gate_silu * up_part).astype(bf16)
        result = (
            jnp.einsum("tf,df->td", activation, down_full, preferred_element_type=f32)
            .astype(bf16)
            .astype(f32)
        )
        part_out = part_out + gate * result
        dots = jnp.sum(cot_rows * result, axis=1, keepdims=True)
        dots_high = dots.astype(bf16).astype(f32)
        part_dots = part_dots + jnp.where(
            (lane == number)[None, :],
            dots_high,
            jnp.where((lane == number + experts)[None, :], dots - dots_high, 0.0),
        )
        result_grad = (gate * cot_rows).astype(bf16)
        activation_grad = jnp.dot(result_grad, down_full, preferred_element_type=f32)
        inner_grad = jnp.concatenate(
            [
                activation_grad * up_part * gate_sigmoid * (1.0 + gate_part * (1.0 - gate_sigmoid)),
                activation_grad * gate_silu,
            ],
            axis=-1,
        ).astype(bf16)
        part_back = part_back + jnp.einsum(
            "tf,df->td", inner_grad, in_full, preferred_element_type=f32
        )
        in_grad = jnp.einsum("td,tf->df", group_normed, inner_grad, preferred_element_type=f32)
        down_grad = jnp.einsum("td,tf->df", result_grad, activation, preferred_element_type=f32)
        expert_grads.append(
            jnp.concatenate([in_grad.astype(bf16), down_grad.astype(bf16)], axis=1)
        )
    parts = jnp.concatenate(
        [part_out.astype(bf16), part_back.astype(bf16), part_dots.astype(bf16)], axis=1
    )
    parts = collect(parts, "core").astype(bf16).reshape(n_a, rows, 2 * width + LANES)
    parts = lax.all_to_all(parts, "a", split_axis=0, concat_axis=0, tiled=True)

    expert_grad = jnp.stack(expert_grads).reshape(n_e * n_r, n_c * n_a, width // (n_r * n_c * n_a), 3 * FF)
    expert_grad = collect(expert_grad, ("exp", "r")).astype(bf16)
    expert_grad = lax.all_to_all(
        expert_grad.reshape((local_count,) + expert_grad.shape[-2:]),
        ("core", "a"),
        split_axis=0,
        concat_axis=0,
        tiled=True,
    ).astype(f32)
    d_in = expert_grad[:, :, : 2 * FF]
    d_down = expert_grad[:, :, 2 * FF :]

    back = reorder_matrix(expert, dense)
    mixed = jnp.einsum("std,de->te", parts[:, :, :width], back, preferred_element_type=f32)
    copies_grad = jnp.einsum(
        "std,de->te", parts[:, :, width : 2 * width], back, preferred_element_type=f32
    )
    dots = jnp.sum(parts[:, :, 2 * width :].astype(f32), axis=0)
    gate_grad = dots[:, :experts] + dots[:, experts : 2 * experts]
    from_dense = reorder_matrix(dense, home)
    block_out = jnp.dot(
        (hidden + mixed).astype(bf16), from_dense, preferred_element_type=f32
    ).astype(bf16)
    logit_grad = (
        gates * (gate_grad - jnp.sum(gates * gate_grad, axis=-1, keepdims=True))
    ).astype(bf16)
    normed_two_grad = copies_grad + jnp.einsum(
        "te,de->td", logit_grad, router_full, preferred_element_type=f32
    )
    scaled_two = normed_two_grad * second_gain
    second_gain_grad = jnp.sum(normed_two_grad * hidden * second_scale, axis=0)
    hidden_grad = (
        upstream
        + second_scale * scaled_two
        - hidden * second_scale**3 * jnp.mean(scaled_two * hidden, axis=-1, keepdims=True)
    )
    branch_grad = hidden_grad.astype(bf16)
    out_grad = jnp.einsum("td,th->dh", branch_grad, attended, preferred_element_type=f32)
    router_grad = jnp.einsum("td,te->de", normed_two, logit_grad, preferred_element_type=f32)
    out_total = reduce_dense(
        jnp.concatenate(
            [
                out_grad.astype(bf16),
                router_grad.astype(bf16),
                second_gain_grad.astype(bf16)[:, None],
                jnp.zeros((width, LANES - experts - 1), bf16),
            ],
            axis=1,
        )
    )
    d_out = out_total[:, :query_width]
    d_router = out_total[:, query_width : query_width + experts]

    attended_grad = (
        jnp.einsum("td,dh->th", branch_grad, out_full, preferred_element_type=f32)
        .astype(bf16)
        .reshape(rows, KEY_VALUE_HEADS, fold, HEAD_DIMENSION)
    )
    value_grad = jnp.einsum(
        "kgts,tkgd->skd", weights.astype(bf16), attended_grad, preferred_element_type=f32
    )
    weight_grad = jnp.einsum(
        "tkgd,skd->kgts", attended_grad, value_rows, preferred_element_type=f32
    )
    row_delta = jnp.sum(weights * weight_grad, axis=-1, keepdims=True)
    score_grad = (weights * (weight_grad - row_delta)).astype(bf16)
    query_grad = (
        jnp.einsum("kgts,skd->tkgd", score_grad, key_rows, preferred_element_type=f32) * score_scale
    )
    key_grad = (
        jnp.einsum("kgts,tkgd->skd", score_grad, query_rows, preferred_element_type=f32)
        * score_scale
    )
    query_grad = rotate_back(
        query_grad.reshape(rows, QUERY_HEADS, HEAD_DIMENSION), cosine_table, sine_table
    ).reshape(rows, query_width)
    key_grad = rotate_back(key_grad, cosine_table, sine_table).reshape(rows, key_width)
    projected_grad = jnp.concatenate(
        [query_grad, key_grad, value_grad.reshape(rows, key_width)], axis=-1
    ).astype(bf16)
    qkv_grad = jnp.einsum("td,tf->df", normed, projected_grad, preferred_element_type=f32)
    normed_grad = jnp.einsum("tf,df->td", projected_grad, qkv_full, preferred_element_type=f32)
    scaled_one = normed_grad * first_gain
    first_gain_grad = jnp.sum(normed_grad * residual * first_scale, axis=0)
    qkv_total = reduce_dense(
        jnp.concatenate(
            [
                qkv_grad.astype(bf16),
                first_gain_grad.astype(bf16)[:, None],
                jnp.zeros((width, LANES - 1), bf16),
            ],
            axis=1,
        )
    )
    d_qkv = qkv_total[:, :qkv_width]
    d_gains = jnp.concatenate(
        [
            qkv_total[:, qkv_width : qkv_width + 1],
            out_total[:, query_width + experts : query_width + experts + 1],
        ],
        axis=1,
    )
    input_grad = (
        hidden_grad
        + first_scale * scaled_one
        - residual * first_scale**3 * jnp.mean(scaled_one * residual, axis=-1, keepdims=True)
    ).astype(bf16)
    input_grad = jnp.dot(input_grad, from_dense, preferred_element_type=f32).astype(bf16)
    new_qkv, new_qkv_mean, new_qkv_square = adamw(
        qkv_weight, d_qkv, qkv_mean, qkv_square, 0.15, decay_rate
    )
    new_out, new_out_mean, new_out_square = adamw(
        out_weight, d_out, out_mean, out_square, 0.3, decay_rate
    )
    new_router, new_router_mean, new_router_square = adamw(
        router_weight, d_router, router_mean, router_square, 0.05, decay_rate
    )
    new_gains, new_gains_mean, new_gains_square = adamw(
        norm_gains, d_gains, gains_mean, gains_square, 0.8, 0.0
    )
    new_in, new_in_mean, new_in_square = adamw(in_weight, d_in, in_mean, in_square, 0.1, decay_rate)
    new_down, new_down_mean, new_down_square = adamw(
        down_weight, d_down, down_mean, down_square, 1.0, decay_rate
    )
    return (
        block_out,
        input_grad,
        new_qkv,
        new_qkv_mean,
        new_qkv_square,
        new_out,
        new_out_mean,
        new_out_square,
        new_router,
        new_router_mean,
        new_router_square,
        new_gains,
        new_gains_mean,
        new_gains_square,
        new_in,
        new_in_mean,
        new_in_square,
        new_down,
        new_down_mean,
        new_down_square,
    )


def solution(mesh):
    n_dp, n_exp = mesh.shape["dp"], mesh.shape["exp"]
    n_a = EXPERTS // n_exp // 2
    mesh = Mesh(
        mesh.devices.reshape(n_a, n_dp // (2 * n_a), 2, n_exp), ("a", "r", "core", "exp")
    )
    placed = (
        P(("a", "r", "core", "exp"), None),
        P(("a", "r", "core", "exp"), None),
        P(("a", "r", "core", "exp"), None),
        P(("a", "r", "core", "exp"), None),
        P(("a", "r", "core", "exp"), None),
        P(("a", "r", "core", "exp"), None),
        P(("a", "r", "core", "exp"), None),
        P(("a", "r", "core", "exp"), None),
        P(("a", "r", "core", "exp"), None),
        P(("a", "r", "core", "exp"), None),
        P(("a", "r", "core", "exp"), None),
        P(("a", "r", "core", "exp"), None),
        P(("a", "r", "core", "exp"), None),
        P(("a", "r", "core", "exp"), None),
        P(("a", "r", "core", "exp"), None),
        P(("a", "r", "core", "exp"), None),
        P("exp", ("a", "r", "core"), None),
        P("exp", ("a", "r", "core"), None),
        P("exp", ("a", "r", "core"), None),
        P("exp", ("a", "r", "core"), None),
        P("exp", ("a", "r", "core"), None),
        P("exp", ("a", "r", "core"), None),
    )
    return jax.shard_map(
        body,
        mesh=mesh,
        in_specs=placed,
        out_specs=(
            P(("a", "r", "core", "exp"), None),
            P(("a", "r", "core", "exp"), None),
            P(("a", "r", "core", "exp"), None),
            P(("a", "r", "core", "exp"), None),
            P(("a", "r", "core", "exp"), None),
            P(("a", "r", "core", "exp"), None),
            P(("a", "r", "core", "exp"), None),
            P(("a", "r", "core", "exp"), None),
            P(("a", "r", "core", "exp"), None),
            P(("a", "r", "core", "exp"), None),
            P(("a", "r", "core", "exp"), None),
            P(("a", "r", "core", "exp"), None),
            P(("a", "r", "core", "exp"), None),
            P(("a", "r", "core", "exp"), None),
            P("exp", ("a", "r", "core"), None),
            P("exp", ("a", "r", "core"), None),
            P("exp", ("a", "r", "core"), None),
            P("exp", ("a", "r", "core"), None),
            P("exp", ("a", "r", "core"), None),
            P("exp", ("a", "r", "core"), None),
        ),
        check_vma=False,
    )
```

time: 1430 us -> 647 us (0.45)
  waiting for transfers between devices: 1010 us -> 216 us
  matrix products: 124 us -> 93.7 us
  starting transfers between devices: 31.7 us -> 54.2 us
  local copies, waits for them, and re-layouts: 52.4 us -> 71.5 us
    reduce_scatter x4 -> x0, waiting for transfers between devices: 604 us -> none  [the longest x1 181 us: body(): lax.psum_scatter(qkv_grad, ('dp', 'exp'), scatter_dimension=0, tiled=True)]
    unnamed x12 -> x2, waiting for transfers between devices: 231 us -> 0.03 us
    all_to_all x8 -> x13, waiting for transfers between devices: 52.7 us -> 216 us  [the longest x6 100 us: spread(): return lax.all_to_all(copies, axes, split_axis=0, concat_axis=0, tiled=True)]
    all_gather x2 -> x0, blocking collectives: 134 us -> none  [the longest x1 69.3 us: body(): lax.all_gather(norm_gains.astype(jnp.bfloat16), ('dp', 'exp'), axis=0, ti...]
    all_to_all x0 -> x6, blocking collectives: none -> 127 us  [the longest x1 54.1 us: body(): parts = lax.all_to_all(parts, 'a', split_axis=0, concat_axis=0, tiled=True)]
    all_gather x4 -> x2, waiting for transfers between devices: 123 us -> 0.01 us  [the longest x1 0.01 us: body(): lax.all_gather(expert_pack, ('exp', 'r'), axis=0, tiled=True)]
    dot_general x36 -> x34, matrix products: 123 us -> 93.7 us  [the longest x2 16.2 us: body(): jnp.einsum('tf,df->td', inner_grad, in_full, preferred_element_type=f32)]
    gather x8 -> x0, local copies, waits for them, and re-layouts: 23 us -> none  [the longest x2 6.93 us: micro_step(): pair_grad[pair_of_slot]]
  transfers between devices with their start and end apart: 18 -> 15, of which waited for: 15 -> 10; matrix products, arithmetic and copies ran while one was open for 9% -> 22% of each run, Pallas kernels for 0% -> 0%
where the time goes in v1:
time: 647 us; the launch traced here: 636 us
  waiting for transfers between devices  216 us (33%)
  blocking collectives  127 us (20%)
  matrix products  93.7 us (14%)
  local copies, waits for them, and re-layouts  71.5 us (11%)
  other arithmetic  58.4 us (9%)
  starting transfers between devices  54.2 us (8%)
  between operations  16 us (2%)
    all_to_all x6, waiting for transfers between devices, spread(): return lax.all_to_all(copies, axes, split_axis=0, concat_axis=0, tiled=True)  100 us
    all_to_all x6, waiting for transfers between devices, collect(): parts = lax.all_to_all(parts, axes, split_axis=0, concat_axis=0, tiled=True)  88 us
    all_to_all x1, blocking collectives, body(): parts = lax.all_to_all(parts, 'a', split_axis=0, concat_axis=0, tiled=True)  54.1 us
    all_to_all x1, blocking collectives, body(): lax.all_to_all(expert_pack, ('core', 'a'), split_axis=0, concat_axis=0, t...  43.8 us
    all_to_all x1, waiting for transfers between devices, body(): lax.all_to_all(expert_grad.reshape((local_count,) + expert_grad.shape[-2:...  27.4 us
    all_to_all x6, starting transfers between devices, collect(): parts = lax.all_to_all(parts, axes, split_axis=0, concat_axis=0, tiled=True)  27.2 us
    all_to_all x6, starting transfers between devices, spread(): return lax.all_to_all(copies, axes, split_axis=0, concat_axis=0, tiled=True)  22.3 us
    reduce_sum x8, other arithmetic, collect(): return jnp.sum(parts.astype(jnp.float32), axis=0)  21.4 us
  transfers between devices with their start and end apart: 15, of which 10 were waited for; matrix products, arithmetic and copies ran while one was open for 22% of the time, Pallas kernels for 0%

profile of v1, /device:TPU:0, one launch (start us, length us, event | category | flops | bytes accessed | tf_op | source)
XLA Modules:
  0.0 636.3 jit_solution(3468711843998783667)
XLA Ops:
  10.5 43.8 %all_to_all.95 = bf16[8,64,1536]{2,1,0:T(8,128)(2,1)} all-to-all(bf16[8,64,1536]{2,1,0:T(8,128)(2,1)S(1)} %pad_maximum_fusion.4), channel_id=1, replica_groups=mesh['a'=4,'r'=2,'core'=2,'exp'=2] {'core','a'}, dimensions={0} | all-to-all | bytes 3145728 | tf_op jit(solution)/shard_map/all_to_all | solution.py:172
  59.1 15.7 %all-to-all-done = bf16[4,32,2176]{2,1,0:T(8,128)(2,1)S(1)} async-done(((bf16[4,32,2176]{2,1,0:T(8,128)(2,1)}), bf16[4,32,2176]{2,1,0:T(8,128)(2,1)S(1)}, u32[]{:S(2)}, u32[]{:S(2)}) %all-to-all-start) | async-done | bytes 557088 | tf_op jit(solution)/shard_map/all_to_all | solution.py:98
  79.3 8.3 %all-to-all-done.3 = bf16[4,32,1024]{2,1,0:T(8,128)(2,1)S(1)} async-done(((bf16[4,32,1024]{2,1,0:T(8,128)(2,1)}), bf16[4,32,1024]{2,1,0:T(8,128)(2,1)S(1)}, u32[]{:S(2)}, u32[]{:S(2)}) %all-to-all-start.3) | async-done | bytes 262176 | tf_op jit(solution)/shard_map/all_to_all | solution.py:98
  97.8 45.9 %all-to-all-done.1 = bf16[4,128,2176]{1,2,0:T(8,128)(2,1)S(1)} async-done(((bf16[4,128,2176]{1,2,0:T(8,128)(2,1)}), bf16[4,128,2176]{1,2,0:T(8,128)(2,1)S(1)}, u32[]{:S(2)}, u32[]{:S(2)}) %all-to-all-start.1) | async-done | bytes 2228256 | tf_op jit(solution)/shard_map/all_to_all | solution.py:98
  160.1 8.5 %all_to_all.96 = bf16[2,512,2176]{1,2,0:T(8,128)(2,1)} all-to-all(bf16[2,512,2176]{1,2,0:T(8,128)(2,1)S(1)} %broadcast_in_dim.199), channel_id=1, replica_groups=mesh['a'=4,'r'=2,'core'=2,'exp'=2] {'core'}, dimensions={0} | all-to-all | bytes 8912896 | tf_op jit(solution)/shard_map/all_to_all | solution.py:98
  174.0 6.6 %copy.417 = bf16[2,512,2176]{2,1,0:T(8,128)(2,1)} copy(bf16[2,512,2176]{1,2,0:T(8,128)(2,1)} %all_to_all.96) | data formatting | bytes 8912896 | tf_op jit(solution)/shard_map/all_to_all | solution.py:98
  210.4 4.3 all-to-all-start.6
  216.4 27.8 %all-to-all-done.6 = bf16[4,128,1152]{1,2,0:T(8,128)(2,1)} async-done(((bf16[4,128,1152]{1,2,0:T(8,128)(2,1)}), bf16[4,128,1152]{1,2,0:T(8,128)(2,1)}, u32[]{:S(2)}, u32[]{:S(2)}) %all-to-all-start.6) | async-done | bytes 1179680 | tf_op jit(solution)/shard_map/all_to_all | solution.py:98
  250.4 5.6 all_to_all.97
  258.6 6.7 %fusion.42 = f32[1024,1024]{0,1:T(8,128)} fusion(bf16[2,1024,1536]{2,1,0:T(8,128)(2,1)} %bitcast.195, bf16[1024,1152]{0,1:T(8,128)(2,1)} %bitcast.161), kind=kOutput, calls=%fused_computation.78 | convolution fusion | flops 2147483648 | bytes 8388608 | tf_op jit(solution)/shard_map/dot_general | solution.py:256
  265.3 5.9 fusion.41
  271.3 5.4 multiply_convert_fusion.1
  285.8 13.9 %fusion.40 = f32[1024,1024]{0,1:T(8,128)S(1)} fusion(bf16[2,1024,1536]{2,1,0:T(8,128)(2,1)S(1)} %bitcast.203, bf16[1024,512]{0,1:T(8,128)(2,1)S(1)} %get-tuple-element.215, bf16[1024,512]{0,1:T(8,128)(2,1)S(1)} %get-tuple-element.214), kind=kOutput, calls=%fused_computation.76 | convolution fusion | flops 2151677952 | bytes 8388608 | tf_op jit(solution)/shard_map/tf,df->td/dot_general | solution.py:284
  303.3 8.4 %all_to_all.98 = bf16[2,512,2176]{1,2,0:T(8,128)(2,1)} all-to-all(bf16[2,512,2176]{1,2,0:T(8,128)(2,1)S(1)} %bitcast.152), channel_id=1, replica_groups=mesh['a'=4,'r'=2,'core'=2,'exp'=2] {'core'}, dimensions={0} | all-to-all | bytes 8912896 | tf_op jit(solution)/shard_map/all_to_all | solution.py:104
  311.6 5.2 reduce_sum.271
  318.8 54.1 %all_to_all.99 = bf16[4,128,2176]{1,2,0:T(8,128)(2,1)S(1)} all-to-all(bf16[4,128,2176]{1,2,0:T(8,128)(2,1)S(1)} %copy_bitcast_fusion.1), channel_id=1, replica_groups=mesh['a'=4,'r'=2,'core'=2,'exp'=2] {'a'}, dimensions={0} | all-to-all | bytes 4456448 | tf_op jit(solution)/shard_map/all_to_all | solution.py:296
  394.4 6.5 %all_to_all.100 = bf16[2,512,1152]{2,1,0:T(8,128)(2,1)} all-to-all(bf16[2,512,1152]{2,1,0:T(8,128)(2,1)S(1)} %concatenate.85), channel_id=1, replica_groups=mesh['a'=4,'r'=2,'core'=2,'exp'=2] {'core'}, dimensions={0} | all-to-all | bytes 4718592 | tf_op jit(solution)/shard_map/all_to_all | solution.py:104
  408.2 4.3 multiply_reduce_fusion.2
  416.3 7.8 %concatenate.82 = bf16[2,512,2176]{2,1,0:T(8,128)(2,1)} concatenate(bf16[2,512,2048]{2,1,0:T(8,128)(2,1)} %bitcast.142, bf16[2,512,1]{2,1,0:T(8,128)(2,1)S(1)} %convert_element_type.335, bf16[2,512,127]{2,1,0:T(8,128)(2,1)S(1)} %broadcast_in_dim.223), dimensions={2} | concatenate | bytes 8912896 | tf_op jit(solution)/shard_map/concatenate | solution.py:383
  424.1 5.7 all-to-all-start.11
  438.1 6.0 convolution_convert_fusion.3
  446.4 5.1 reduce_sum.280
  467.4 8.6 %copy.450 = bf16[2,1024,1536]{2,1,0:T(8,128)(2,1)} copy(bf16[2,1024,1536]{1,2,0:T(8,128)(2,1)} %pad_maximum_fusion) | data formatting | bytes 12582912 | tf_op jit(solution)/shard_map/stack | solution.py:298
  476.0 6.9 %all-to-all-done.12 = bf16[4,128,2176]{2,1,0:T(8,128)(2,1)S(1)} async-done(((bf16[4,128,2176]{2,1,0:T(8,128)(2,1)}), bf16[4,128,2176]{2,1,0:T(8,128)(2,1)S(1)}, u32[]{:S(2)}, u32[]{:S(2)}) %all-to-all-start.12) | async-done | bytes 2228256 | tf_op jit(solution)/shard_map/all_to_all | solution.py:104
  482.9 5.3 all-to-all-start.17
  489.5 68.7 %all-to-all-done.17 = bf16[4,1,8,64,1536]{4,3,2,1,0:T(8,128)(2,1)} async-done(((bf16[4,1,8,64,1536]{4,3,2,1,0:T(8,128)(2,1)}), bf16[4,1,8,64,1536]{4,3,2,1,0:T(8,128)(2,1)}, u32[]{:S(2)}, u32[]{:S(2)}) %all-to-all-start.17) | async-done | bytes 6291488 | tf_op jit(solution)/shard_map/all_to_all | solution.py:104
  558.2 4.8 all-to-all-start.13
  563.0 5.4 reduce_sum.287
  568.4 8.7 %all-to-all-done.13 = bf16[4,32,2176]{2,1,0:T(8,128)(2,1)S(1)} async-done(((bf16[4,32,2176]{2,1,0:T(8,128)(2,1)}), bf16[4,32,2176]{2,1,0:T(8,128)(2,1)S(1)}, u32[]{:S(2)}, u32[]{:S(2)}) %all-to-all-start.13) | async-done | bytes 557088 | tf_op jit(solution)/shard_map/all_to_all | solution.py:104
  577.1 4.6 all-to-all-start.18
  591.6 27.4 %all-to-all-done.18 = bf16[8,64,1536]{2,1,0:T(8,128)(2,1)} async-done(((bf16[8,64,1536]{2,1,0:T(8,128)(2,1)}), bf16[8,64,1536]{2,1,0:T(8,128)(2,1)}, u32[]{:S(2)}, u32[]{:S(2)}) %all-to-all-start.18) | async-done | bytes 1572896 | tf_op jit(solution)/shard_map/all_to_all | solution.py:300
  621.1 5.7 multiply_subtract_fusion
  (372 shorter events, 172.7 us)
Async XLA Ops:
  7.2 86.0 %copy-start = (bf16[128,1024]{1,0:T(8,128)(2,1)S(1)}, bf16[128,1024]{1,0:T(8,128)(2,1)}, u32[]{:S(2)}) copy-start(bf16[128,1024]{1,0:T(8,128)(2,1)} %param.26) | copy-start | bytes 786436
  7.2 251.4 %all-gather.3.cloned.1.call-start = ((), (), s32[]{:S(2)}) async-start(), calls=%async_computation.19 | async-start | bytes 7864320 | tf_op jit(solution)/shard_map/all_gather | solution.py:173
  10.5 43.9 %copy-start.22 = (f32[32,2048]{1,0:T(8,128)S(1)}, f32[32,2048]{1,0:T(8,128)}, u32[]{:S(2)}) copy-start(f32[32,2048]{1,0:T(8,128)} %param.29) | copy-start | bytes 786436
  10.5 43.9 %copy-start.55 = (f32[32,16]{0,1:T(8,128)S(1)}, f32[32,16]{0,1:T(8,128)}, u32[]{:S(2)}) copy-start(f32[32,16]{0,1:T(8,128)} %param.35) | copy-start | bytes 6148
  10.5 44.0 %copy-start.80 = (f32[32,2]{0,1:T(2,128)S(1)}, f32[32,2]{0,1:T(2,128)}, u32[]{:S(2)}) copy-start(f32[32,2]{0,1:T(2,128)} %param.38) | copy-start | bytes 772
  55.6 19.3 %all-to-all-start = ((bf16[4,32,2176]{2,1,0:T(8,128)(2,1)}), bf16[4,32,2176]{2,1,0:T(8,128)(2,1)S(1)}, u32[]{:S(2)}, u32[]{:S(2)}) async-start(bf16[4,32,2176]{2,1,0:T(8,128)(2,1)} %broadcast_in_dim.195), calls=%async_computation | async-start | bytes 1114112 | tf_op jit(solution)/shard_map/all_to_all | solution.py:98
  75.6 12.0 %all-to-all-start.3 = ((bf16[4,32,1024]{2,1,0:T(8,128)(2,1)}), bf16[4,32,1024]{2,1,0:T(8,128)(2,1)S(1)}, u32[]{:S(2)}, u32[]{:S(2)}) async-start(bf16[4,32,1024]{2,1,0:T(8,128)(2,1)} %broadcast_in_dim.202), calls=%async_computation.3 | async-start | bytes 524288 | tf_op jit(solution)/shard_map/all_to_all | solution.py:98
  89.3 54.4 %all-to-all-start.1 = ((bf16[4,128,2176]{1,2,0:T(8,128)(2,1)}), bf16[4,128,2176]{1,2,0:T(8,128)(2,1)S(1)}, u32[]{:S(2)}, u32[]{:S(2)}) async-start(bf16[4,128,2176]{1,2,0:T(8,128)(2,1)} %broadcast_in_dim.197), calls=%async_computation.1 | async-start | bytes 4456448 | tf_op jit(solution)/shard_map/all_to_all | solution.py:98
  93.2 178.1 %all-gather.5.cloned.1.call-start = ((), (), s32[]{:S(2)}) async-start(), calls=%async_computation.20 | async-start | bytes 2359296 | tf_op jit(solution)/shard_map/all_gather | solution.py:170
  97.8 50.5 %copy-start.71 = (s32[128,8]{0,1:T(8,128)S(1)}, s32[128,8]{0,1:T(8,128)}, u32[]{:S(2)}) copy-start(s32[128,8]{0,1:T(8,128)} %param.28) | copy-start | bytes 12292
  144.8 15.0 %all-to-all-start.4 = ((bf16[4,128,1024]{2,1,0:T(8,128)(2,1)}), bf16[4,128,1024]{2,1,0:T(8,128)(2,1)S(1)}, u32[]{:S(2)}, u32[]{:S(2)}) async-start(bf16[4,128,1024]{2,1,0:T(8,128)(2,1)} %broadcast_in_dim.204), calls=%async_computation.4 | async-start | bytes 2097152 | tf_op jit(solution)/shard_map/all_to_all | solution.py:98
  170.1 22.4 %all-to-all-start.5 = ((bf16[2,512,1024]{2,1,0:T(8,128)(2,1)}), bf16[2,512,1024]{2,1,0:T(8,128)(2,1)S(1)}, u32[]{:S(2)}, u32[]{:S(2)}) async-start(bf16[2,512,1024]{2,1,0:T(8,128)(2,1)} %broadcast_in_dim.206), calls=%async_computation.5 | async-start | bytes 4194304 | tf_op jit(solution)/shard_map/all_to_all | solution.py:98
  173.9 8.7 %copy-start.3 = (f32[128,1024]{0,1:T(8,128)S(1)}, f32[128,1024]{0,1:T(8,128)}, u32[]{:S(2)}) copy-start(f32[128,1024]{0,1:T(8,128)} %get-tuple-element.240) | copy-start | bytes 1572868
  173.9 8.7 %copy-start.65 = (f32[128]{0:T(128)S(1)}, f32[128]{0:T(128)}, u32[]{:S(2)}) copy-start(f32[128]{0:T(128)} %get-tuple-element.236) | copy-start | bytes 1540
  210.4 33.8 %all-to-all-start.6 = ((bf16[4,128,1152]{1,2,0:T(8,128)(2,1)}), bf16[4,128,1152]{1,2,0:T(8,128)(2,1)}, u32[]{:S(2)}, u32[]{:S(2)}) async-start(bf16[4,128,1152]{1,2,0:T(8,128)(2,1)} %broadcast_in_dim.210), calls=%async_computation.6 | async-start | bytes 2359296 | tf_op jit(solution)/shard_map/all_to_all | solution.py:98
  271.3 8.9 %copy-start.97 = (f32[1024,1024]{0,1:T(8,128)S(1)}, f32[1024,1024]{0,1:T(8,128)}, u32[]{:S(2)}) copy-start(f32[1024,1024]{0,1:T(8,128)} %fusion.41) | copy-start | bytes 12582916
  276.6 23.1 %copy-start.106 = (bf16[1024,512]{0,1:T(8,128)(2,1)}, bf16[1024,512]{0,1:T(8,128)(2,1)S(1)}, u32[]{:S(2)}) copy-start(bf16[1024,512]{0,1:T(8,128)(2,1)S(1)} %get-tuple-element.212) | copy-start | bytes 3145732
  276.7 23.0 %copy-start.107 = (bf16[1024,512]{0,1:T(8,128)(2,1)}, bf16[1024,512]{0,1:T(8,128)(2,1)S(1)}, u32[]{:S(2)}) copy-start(bf16[1024,512]{0,1:T(8,128)(2,1)S(1)} %get-tuple-element.213) | copy-start | bytes 3145732
  401.0 7.2 %copy-start.28 = (bf16[128,16,32]{0,2,1:T(8,128)(2,1)S(1)}, bf16[128,16,32]{0,2,1:T(8,128)(2,1)}, u32[]{:S(2)}) copy-start(bf16[128,16,32]{0,2,1:T(8,128)(2,1)} %get-tuple-element.220) | copy-start | bytes 393220
  404.4 19.6 %all-to-all-start.15 = ((bf16[4,128,1152]{2,1,0:T(8,128)(2,1)}), bf16[4,128,1152]{2,1,0:T(8,128)(2,1)S(1)}, u32[]{:S(2)}, u32[]{:S(2)}) async-start(bf16[4,128,1152]{2,1,0:T(8,128)(2,1)} %bitcast.158), calls=%async_computation.15 | async-start | bytes 2359296 | tf_op jit(solution)/shard_map/all_to_all | solution.py:104
  424.1 10.3 %all-to-all-start.11 = ((bf16[2,512,2176]{2,1,0:T(8,128)(2,1)}), bf16[2,512,2176]{2,1,0:T(8,128)(2,1)}, u32[]{:S(2)}, u32[]{:S(2)}) async-start(bf16[2,512,2176]{2,1,0:T(8,128)(2,1)} %concatenate.82), calls=%async_computation.11 | async-start | bytes 8912896 | tf_op jit(solution)/shard_map/all_to_all | solution.py:104
  434.4 17.1 %all-to-all-start.16 = ((bf16[4,32,1152]{2,1,0:T(8,128)(2,1)}), bf16[4,32,1152]{2,1,0:T(8,128)(2,1)S(1)}, u32[]{:S(2)}, u32[]{:S(2)}) async-start(bf16[4,32,1152]{2,1,0:T(8,128)(2,1)} %bitcast.52), calls=%async_computation.16 | async-start | bytes 589824 | tf_op jit(solution)/shard_map/all_to_all | solution.py:104
  452.2 30.7 %all-to-all-start.12 = ((bf16[4,128,2176]{2,1,0:T(8,128)(2,1)}), bf16[4,128,2176]{2,1,0:T(8,128)(2,1)S(1)}, u32[]{:S(2)}, u32[]{:S(2)}) async-start(bf16[4,128,2176]{2,1,0:T(8,128)(2,1)} %bitcast.155), calls=%async_computation.12 | async-start | bytes 4456448 | tf_op jit(solution)/shard_map/all_to_all | solution.py:104
  482.9 75.3 %all-to-all-start.17 = ((bf16[4,1,8,64,1536]{4,3,2,1,0:T(8,128)(2,1)}), bf16[4,1,8,64,1536]{4,3,2,1,0:T(8,128)(2,1)}, u32[]{:S(2)}, u32[]{:S(2)}) async-start(bf16[4,1,8,64,1536]{4,3,2,1,0:T(8,128)(2,1)} %bitcast.143), calls=%async_computation.17 | async-start | bytes 12582912 | tf_op jit(solution)/shard_map/all_to_all | solution.py:104
  558.2 18.9 %all-to-all-start.13 = ((bf16[4,32,2176]{2,1,0:T(8,128)(2,1)}), bf16[4,32,2176]{2,1,0:T(8,128)(2,1)S(1)}, u32[]{:S(2)}, u32[]{:S(2)}) async-start(bf16[4,32,2176]{2,1,0:T(8,128)(2,1)} %bitcast.170), calls=%async_computation.13 | async-start | bytes 1114112 | tf_op jit(solution)/shard_map/all_to_all | solution.py:104
  568.4 13.3 %copy-start.7 = (f32[128,1024]{0,1:T(8,128)S(1)}, f32[128,1024]{0,1:T(8,128)}, u32[]{:S(2)}) copy-start(f32[128,1024]{0,1:T(8,128)} %copy-done.5) | copy-start | bytes 1572868
  568.4 13.3 %copy-start.36 = (bf16[128,1024]{0,1:T(8,128)(2,1)S(1)}, bf16[128,1024]{0,1:T(8,128)(2,1)}, u32[]{:S(2)}) copy-start(bf16[128,1024]{0,1:T(8,128)(2,1)} %get-tuple-element.183) | copy-start | bytes 786436
  568.4 13.3 %copy-start.93 = (s32[1024]{0:T(1024)S(1)}, s32[1024]{0:T(1024)}, u32[]{:S(2)}) copy-start(s32[1024]{0:T(1024)} %constant.75.clone) | copy-start | bytes 12292
  568.4 13.3 %copy-start.96 = (s32[1024]{0:T(1024)S(1)}, s32[1024]{0:T(1024)}, u32[]{:S(2)}) copy-start(s32[1024]{0:T(1024)} %constant.76.clone) | copy-start | bytes 12292
  577.1 41.9 %all-to-all-start.18 = ((bf16[8,64,1536]{2,1,0:T(8,128)(2,1)}), bf16[8,64,1536]{2,1,0:T(8,128)(2,1)}, u32[]{:S(2)}, u32[]{:S(2)}) async-start(bf16[8,64,1536]{2,1,0:T(8,128)(2,1)} %reduce_sum.287), calls=%async_computation.18 | async-start | bytes 3145728 | tf_op jit(solution)/shard_map/all_to_all | solution.py:300
  591.6 29.4 %copy-start.2 = (f32[8,64,1024]{2,1,0:T(8,128)S(1)}, f32[8,64,1024]{2,1,0:T(8,128)}, u32[]{:S(2)}) copy-start(f32[8,64,1024]{2,1,0:T(8,128)} %param.41) | copy-start | bytes 6291460
  621.1 7.9 %copy-start.1 = (bf16[128,1024]{1,0:T(8,128)(2,1)S(1)}, bf16[128,1024]{1,0:T(8,128)(2,1)}, u32[]{:S(2)}) copy-start(bf16[128,1024]{1,0:T(8,128)(2,1)} %param.26) | copy-start | bytes 786436
  (93 other events, 284.8 us)
Sparse Core Ops, SparseCore 0:
  54.5 92.4 all-gather.2
  149.2 36.3 all-gather.4

commit v2 on v1

v2 whole, which is shorter than its diff:
```python
import functools
import math

import jax
import jax.numpy as jnp
import numpy as np
from jax import lax
from jax.experimental import pallas as pl
from jax.experimental.pallas import tpu as pltpu
from jax.sharding import Mesh
from jax.sharding import PartitionSpec as P

QUERY_HEADS = 16
KEY_VALUE_HEADS = 8
HEAD_DIMENSION = 64
FF = 512
STEP = 10
EXPERTS = 16
LANES = 128
VMEM_BYTES = 48 * 1024 * 1024


norm_eps = 1e-06
rope_base = 10000.0
mask_fill = -1e30
beta_one = 0.9
beta_two = 0.95
adam_eps = 1e-08
decay_rate = 0.1


def rms_scale(values):
    return lax.rsqrt(jnp.mean(values * values, axis=-1, keepdims=True) + norm_eps)


def doc_layout(doc_lens, sequence_length):
    row_index = jnp.arange(sequence_length, dtype=jnp.int32)
    doc_ends = jnp.cumsum(doc_lens, dtype=jnp.int32)
    passed = (row_index[:, None] >= doc_ends[None, :]).astype(jnp.int32)
    segment = jnp.sum(passed, axis=1, dtype=jnp.int32)
    starts = jnp.sum(passed * doc_lens[None, :], axis=1, dtype=jnp.int32)
    return ((row_index - starts).astype(jnp.float32), segment)


def rope_tables(positions, head_size):
    half_size = head_size // 2
    freq_index = jnp.arange(half_size, dtype=jnp.float32)
    inverse = jnp.exp(freq_index * (-2.0 * math.log(rope_base) / head_size))
    angles = positions[:, None] * inverse[None, :]
    return (jnp.cos(angles), jnp.sin(angles))


def adamw(weight, gradient, mean_old, square_old, step_rate, weight_decay):
    mean_new = beta_one * mean_old + (1.0 - beta_one) * gradient
    square_new = beta_two * square_old + (1.0 - beta_two) * gradient * gradient
    corrected = (
        mean_new
        / (1.0 - beta_one**STEP)
        / (jnp.sqrt(square_new / (1.0 - beta_two**STEP)) + adam_eps)
    )
    return (weight - step_rate * (corrected + weight_decay * weight), mean_new, square_new)

def dot_nn(left, right):
    return jnp.dot(left, right, preferred_element_type=jnp.float32)


def dot_nt(left, right):
    return lax.dot_general(left, right, (((1,), (1,)), ((), ())), preferred_element_type=jnp.float32)


def dot_tn(left, right):
    return lax.dot_general(left, right, (((0,), (0,)), ((), ())), preferred_element_type=jnp.float32)


def lane_iota(rows):
    return lax.broadcasted_iota(jnp.int32, (rows, LANES), 1)


def gain_rows(extra, experts):
    row = lax.broadcasted_iota(jnp.int32, (8, LANES), 0)
    pick = (lane_iota(8) == row + experts).astype(jnp.bfloat16)
    return dot_nt(jnp.where(row < 2, pick, jnp.zeros_like(pick)), extra)


def swap_halves(values):
    half = HEAD_DIMENSION // 2
    lower = lane_iota(values.shape[0]) % HEAD_DIMENSION < half
    return jnp.where(lower, pltpu.roll(values, LANES - half, 1), pltpu.roll(values, half, 1))


def column_sums(values, lane):
    high = values.astype(jnp.bfloat16)
    low = (values - high.astype(jnp.float32)).astype(jnp.bfloat16)
    place = (lane_iota(values.shape[0]) == lane).astype(jnp.bfloat16)
    return dot_tn(high, place) + dot_tn(low, place)


def head_block(index):
    return slice(index * HEAD_DIMENSION, (index + 1) * HEAD_DIMENSION)


def attention_forward(
    experts,
    copies,
    x_ref,
    w_ref,
    cos_ref,
    sin_ref,
    allow_ref,
    used_ref,
    order_ref,
    hidden_ref,
    normed_ref,
    qkv_ref,
    lse_ref,
    att_ref,
    second_ref,
    gates_ref,
    sent_ref,
):
    f32, bf16 = jnp.float32, jnp.bfloat16
    width = x_ref.shape[1]
    rows = x_ref.shape[0]
    qkv_width = qkv_ref.shape[1]
    query_width = QUERY_HEADS * HEAD_DIMENSION
    key_width = KEY_VALUE_HEADS * HEAD_DIMENSION
    extra = w_ref[:, qkv_width + width :]
    gains = gain_rows(extra, experts)
    x = x_ref[...].astype(f32)
    normed = (x * rms_scale(x) * gains[0:1]).astype(bf16)
    normed_ref[...] = normed
    cosine, sine = cos_ref[...], sin_ref[...]
    for start in range(0, qkv_width, 512):
        part = dot_nn(normed, w_ref[:, start : start + 512])
        for inner in range(0, 512, LANES):
            piece = part[:, inner : inner + LANES]
            if start + inner < query_width + key_width:
                piece = piece * cosine + swap_halves(piece) * sine
            qkv_ref[:, start + inner : start + inner + LANES] = piece.astype(bf16)
    allowed = allow_ref[...] > 0.0
    lane = lane_iota(rows)
    logs = jnp.zeros((rows, LANES), f32)
    fold = QUERY_HEADS // KEY_VALUE_HEADS
    for group in range(KEY_VALUE_HEADS):
        keys = qkv_ref[:, query_width + group * HEAD_DIMENSION : query_width + (group + 1) * HEAD_DIMENSION]
        values = qkv_ref[
            :,
            query_width + key_width + group * HEAD_DIMENSION : query_width
            + key_width
            + (group + 1) * HEAD_DIMENSION,
        ]
        outs = []
        for head in range(group * fold, (group + 1) * fold):
            scores = dot_nt(qkv_ref[:, head_block(head)], keys) * HEAD_DIMENSION ** (-0.5)
            scores = jnp.where(allowed, scores, mask_fill)
            peak = jnp.max(scores, axis=1, keepdims=True)
            log_total = peak + jnp.log(jnp.sum(jnp.exp(scores - peak), axis=1, keepdims=True))
            logs = jnp.where(lane == head, log_total, logs)
            outs.append(dot_nn(jnp.exp(scores - log_total).astype(bf16), values))
        att_ref[:, group * fold * HEAD_DIMENSION : (group + 1) * fold * HEAD_DIMENSION] = (
            jnp.concatenate(outs, axis=1).astype(bf16)
        )
    lse_ref[...] = logs
    hidden = x + dot_nt(att_ref[...], w_ref[:, qkv_width : qkv_width + width])
    hidden_ref[...] = hidden
    second = (hidden * rms_scale(hidden) * gains[1:2]).astype(bf16)
    second_ref[...] = second
    used = used_ref[...] > 0.0
    logits = jnp.where(used, dot_nn(second, extra), mask_fill)
    powers = jnp.where(used, jnp.exp(logits - jnp.max(logits, axis=1, keepdims=True)), 0.0)
    gates = powers / jnp.sum(powers, axis=1, keepdims=True)
    gates_ref[...] = gates
    high = gates.astype(bf16).astype(f32)
    lanes = (high + pltpu.roll(gates - high, experts, 1)).astype(bf16)
    moved = dot_nn(second, order_ref[...]).astype(bf16)
    for copy in range(copies):
        sent_ref[copy, :, :width] = moved
        sent_ref[copy, :, width:] = lanes


def experts_forward(
    experts,
    local_count,
    place_ref,
    rows_ref,
    cot_ref,
    w_ref,
    out_ref,
    dots_ref,
    inner_ref,
    sum_ref,
    dots_sum_ref,
):
    f32, bf16 = jnp.float32, jnp.bfloat16
    index, chunk = pl.program_id(0), pl.program_id(1)
    count, width = cot_ref.shape
    number = index * local_count + place_ref[0]
    lane = lane_iota(count)
    chosen = (lane == number) | (lane == number + experts)
    gate = jnp.sum(
        jnp.where(chosen, rows_ref[:, width:].astype(f32), 0.0), axis=1, keepdims=True
    )
    inner = dot_nn(rows_ref[:, :width], w_ref[0, :, : 2 * FF])
    inner_ref[0] = inner
    gate_part = inner[:, :FF]
    activation = (gate_part * jax.nn.sigmoid(gate_part) * inner[:, FF:]).astype(bf16)
    result = dot_nt(activation, w_ref[0, :, 2 * FF :]).astype(bf16).astype(f32)
    dots = jnp.sum(cot_ref[...].astype(f32) * result, axis=1, keepdims=True)
    dots_high = dots.astype(bf16).astype(f32)
    lanes = jnp.where(lane == number, dots_high, 0.0) + jnp.where(
        lane == number + experts, dots - dots_high, 0.0
    )
    here = pl.ds(pl.multiple_of(chunk * count, count), count)

    @pl.when(index == 0)
    def _():
        sum_ref[here, :] = gate * result
        dots_sum_ref[here, :] = lanes

    @pl.when(index > 0)
    def _():
        sum_ref[here, :] += gate * result
        dots_sum_ref[here, :] += lanes

    out_ref[...] = sum_ref[here, :].astype(bf16)
    dots_ref[...] = dots_sum_ref[here, :].astype(bf16)


def experts_backward(
    experts,
    local_count,
    place_ref,
    gates_ref,
    cot_ref,
    w_ref,
    inner_ref,
    dots_ref,
    back_ref,
    inner_grad_ref,
    act_ref,
    result_grad_ref,
    sum_ref,
):
    f32, bf16 = jnp.float32, jnp.bfloat16
    index, chunk = pl.program_id(0), pl.program_id(1)
    count, width = cot_ref.shape
    number = index * local_count + place_ref[0]
    lane = lane_iota(count)
    chosen = (lane == number) | (lane == number + experts)
    gate = jnp.sum(jnp.where(chosen, gates_ref[...].astype(f32), 0.0), axis=1, keepdims=True)
    result_grad = (gate * cot_ref[...].astype(f32)).astype(bf16)
    result_grad_ref[0] = result_grad
    act_grad = dot_nn(result_grad, w_ref[0, :, 2 * FF :])
    gate_part = inner_ref[0, :, :FF]
    up_part = inner_ref[0, :, FF:]
    gate_sigmoid = jax.nn.sigmoid(gate_part)
    gate_silu = gate_part * gate_sigmoid
    act_ref[0] = (gate_silu * up_part).astype(bf16)
    inner_grad_ref[0, :, :FF] = (
        act_grad * up_part * gate_sigmoid * (1.0 + gate_part * (1.0 - gate_sigmoid))
    ).astype(bf16)
    inner_grad_ref[0, :, FF:] = (act_grad * gate_silu).astype(bf16)
    copy_grad = dot_nt(inner_grad_ref[0], w_ref[0, :, : 2 * FF])
    here = pl.ds(pl.multiple_of(chunk * count, count), count)

    @pl.when(index == 0)
    def _():
        sum_ref[here, :] = copy_grad

    @pl.when(index > 0)
    def _():
        sum_ref[here, :] += copy_grad

    back_ref[:, :width] = sum_ref[here, :].astype(bf16)
    back_ref[:, width:] = dots_ref[...]


def experts_weights(rows_ref, inner_grad_ref, result_grad_ref, act_ref, grad_ref):
    grad_ref[0, :, : 2 * FF] = dot_tn(rows_ref[...], inner_grad_ref[0]).astype(jnp.bfloat16)
    grad_ref[0, :, 2 * FF :] = dot_tn(result_grad_ref[0], act_ref[0]).astype(jnp.bfloat16)


def home_backward(
    experts,
    parts_ref,
    order_ref,
    cot_ref,
    hidden_ref,
    second_ref,
    gates_ref,
    w_ref,
    att_ref,
    hidden_grad_ref,
    branch_grad_ref,
    out_grad_ref,
):
    f32, bf16 = jnp.float32, jnp.bfloat16
    rows, width = cot_ref.shape
    sources = parts_ref.shape[0]
    extra = w_ref[:, w_ref.shape[1] - LANES :]
    second_gain = gain_rows(extra, experts)[1:2]
    dots = jnp.zeros((rows, LANES), f32)
    second_grad = jnp.zeros((rows, width), f32)
    for source in range(sources):
        dots = dots + parts_ref[source, :, width:].astype(f32)
        second_grad = second_grad + dot_nn(parts_ref[source, :, :width], order_ref[...])
    dots = dots + pltpu.roll(dots, LANES - experts, 1)
    gates = gates_ref[...]
    logit_grad = (gates * (dots - jnp.sum(gates * dots, axis=1, keepdims=True))).astype(bf16)
    second_grad = second_grad + dot_nt(logit_grad, extra)
    hidden = hidden_ref[...]
    scale = rms_scale(hidden)
    scaled = second_grad * second_gain
    hidden_grad = (
        cot_ref[...].astype(f32)
        + scale * scaled
        - hidden * (scale * scale * scale) * jnp.mean(scaled * hidden, axis=1, keepdims=True)
    )
    hidden_grad_ref[...] = hidden_grad
    branch_grad = hidden_grad.astype(bf16)
    branch_grad_ref[...] = branch_grad
    for start in range(0, width, 512):
        out_grad_ref[:, start : start + 512] = dot_tn(
            branch_grad, att_ref[:, start : start + 512]
        ).astype(bf16)
    out_grad_ref[:, width:] = (
        dot_tn(second_ref[...], logit_grad) + column_sums(second_grad * hidden * scale, experts)
    ).astype(bf16)


def attention_backward(
    experts,
    branch_grad_ref,
    hidden_grad_ref,
    w_ref,
    qkv_ref,
    lse_ref,
    normed_ref,
    x_ref,
    cos_ref,
    sin_ref,
    allow_ref,
    qkv_grad_ref,
    input_grad_ref,
    mid_ref,
    proj_ref,
):
    f32, bf16 = jnp.float32, jnp.bfloat16
    rows, width = x_ref.shape
    qkv_width = qkv_ref.shape[1]
    query_width = QUERY_HEADS * HEAD_DIMENSION
    key_width = KEY_VALUE_HEADS * HEAD_DIMENSION
    fold = QUERY_HEADS // KEY_VALUE_HEADS
    score_scale = HEAD_DIMENSION ** (-0.5)
    first_gain = gain_rows(w_ref[:, qkv_width + width :], experts)[0:1]
    mid_ref[...] = dot_nn(branch_grad_ref[...], w_ref[:, qkv_width : qkv_width + width]).astype(bf16)
    cosine, sine = cos_ref[...], sin_ref[...]
    allowed = allow_ref[...] > 0.0
    lane = lane_iota(rows)
    logs = lse_ref[...]

    def turned_back(values):
        return (values * cosine - swap_halves(values) * sine).astype(bf16)

    key_grads, value_grads = [], []
    for group in range(KEY_VALUE_HEADS):
        keys = qkv_ref[:, query_width + group * HEAD_DIMENSION : query_width + (group + 1) * HEAD_DIMENSION]
        values = qkv_ref[
            :,
            query_width + key_width + group * HEAD_DIMENSION : query_width
            + key_width
            + (group + 1) * HEAD_DIMENSION,
        ]
        query_grads = []
        key_grad = jnp.zeros((rows, HEAD_DIMENSION), f32)
        value_grad = jnp.zeros((rows, HEAD_DIMENSION), f32)
        for head in range(group * fold, (group + 1) * fold):
            queries = qkv_ref[:, head_block(head)]
            mid = mid_ref[:, head_block(head)]
            log_total = jnp.sum(jnp.where(lane == head, logs, 0.0), axis=1, keepdims=True)
            scores = jnp.where(allowed, dot_nt(queries, keys) * score_scale, mask_fill)
            weights = jnp.exp(scores - log_total)
            weight_grad = dot_nt(mid, values)
            delta = jnp.sum(weights * weight_grad, axis=1, keepdims=True)
            score_grad = (weights * (weight_grad - delta)).astype(bf16)
            query_grads.append(dot_nn(score_grad, keys) * score_scale)
            key_grad = key_grad + dot_tn(score_grad, queries)
            value_grad = value_grad + dot_tn(weights.astype(bf16), mid)
        proj_ref[:, group * LANES : (group + 1) * LANES] = turned_back(
            jnp.concatenate(query_grads, axis=1)
        )
        key_grads.append(key_grad * score_scale)
        value_grads.append(value_grad)
        if group % 2 == 1:
            start = query_width + (group // 2) * LANES
            proj_ref[:, start : start + LANES] = turned_back(
                jnp.concatenate(key_grads[-2:], axis=1)
            )
            start = start + key_width
            proj_ref[:, start : start + LANES] = jnp.concatenate(value_grads[-2:], axis=1).astype(
                bf16
            )
    normed = normed_ref[...]
    for start in range(0, qkv_width, 512):
        qkv_grad_ref[:, start : start + 512] = dot_tn(
            normed, proj_ref[:, start : start + 512]
        ).astype(bf16)
    normed_grad = dot_nt(proj_ref[...], w_ref[:, :qkv_width])
    x = x_ref[...].astype(f32)
    scale = rms_scale(x)
    scaled = normed_grad * first_gain
    qkv_grad_ref[:, qkv_width:] = column_sums(normed_grad * x * scale, 0).astype(bf16)
    input_grad_ref[...] = (
        hidden_grad_ref[...]
        + scale * scaled
        - x * (scale * scale * scale) * jnp.mean(scaled * x, axis=1, keepdims=True)
    ).astype(bf16)


def whole_call(kernel, outputs, operands, flops, scratch=()):
    moved = sum(math.prod(item.shape) * item.dtype.itemsize for item in list(outputs) + list(operands))
    return pl.pallas_call(
        kernel,
        out_shape=outputs,
        in_specs=[pl.BlockSpec(memory_space=pltpu.VMEM)] * len(operands),
        out_specs=[pl.BlockSpec(memory_space=pltpu.VMEM)] * len(outputs),
        scratch_shapes=list(scratch),
        compiler_params=pltpu.CompilerParams(vmem_limit_bytes=VMEM_BYTES),
        cost_estimate=pl.CostEstimate(flops=flops, bytes_accessed=moved, transcendentals=0),
    )(*operands)


def order_of(kind, sizes):
    axes = {"home": (0, 1, 2, 3, 4), "dense": (2, 1, 3, 0, 4), "expert": (1, 2, 0, 3, 4)}[kind]
    return np.arange(math.prod(sizes), dtype=np.int32).reshape(sizes).transpose(axes).reshape(-1)


def reorder_matrix(before, after):
    return (jnp.asarray(before)[:, None] == jnp.asarray(after)[None, :]).astype(jnp.bfloat16)


def exchange(values, axes):
    return lax.all_to_all(values, axes, split_axis=0, concat_axis=0, tiled=True)


def spread(values, axes):
    count = lax.axis_size(axes)
    copies = exchange(jnp.broadcast_to(values[None], (count,) + values.shape), axes)
    return copies.reshape((count * values.shape[0],) + values.shape[1:])


def collect(values, axes):
    count = lax.axis_size(axes)
    parts = exchange(values.reshape((count, values.shape[0] // count) + values.shape[1:]), axes)
    total = parts[0].astype(jnp.float32)
    for index in range(1, count):
        total = total + parts[index].astype(jnp.float32)
    return total


def reduce_dense(grad):
    grad = collect(grad, "core").astype(jnp.bfloat16)
    grad = collect(grad, ("r", "exp")).astype(jnp.bfloat16)
    return collect(grad, "a")


def run_experts(place, arrived, cot_group, expert_full, experts, local_count):
    f32, bf16 = jnp.float32, jnp.bfloat16
    shape = jax.ShapeDtypeStruct
    n_e, width, _ = expert_full.shape
    group_rows = arrived.shape[0]
    count = min(256, group_rows)
    chunks = group_rows // count
    params = pltpu.CompilerParams(vmem_limit_bytes=VMEM_BYTES)
    scalar = pl.BlockSpec(memory_space=pltpu.SMEM)
    cot_spec = pl.BlockSpec((count, width), lambda k, i: (i, 0))
    w_spec = pl.BlockSpec((1, width, 3 * FF), lambda k, i: (k, 0, 0))
    inner_spec = pl.BlockSpec((1, count, 2 * FF), lambda k, i: (k, i, 0))
    dots_spec = pl.BlockSpec((count, LANES), lambda k, i: (i, 0))
    rows_spec = pl.BlockSpec((count, width + LANES), lambda k, i: (i, 0))
    flops = 2 * n_e * group_rows * width * 3 * FF
    weight_bytes = n_e * width * 3 * FF * 2
    out, dots, inner = pl.pallas_call(
        functools.partial(experts_forward, experts, local_count),
        grid=(n_e, chunks),
        out_shape=[
            shape((group_rows, width), bf16),
            shape((group_rows, LANES), bf16),
            shape((n_e, group_rows, 2 * FF), f32),
        ],
        in_specs=[scalar, rows_spec, cot_spec, w_spec],
        out_specs=[cot_spec, dots_spec, inner_spec],
        scratch_shapes=[pltpu.VMEM((group_rows, width), f32), pltpu.VMEM((group_rows, LANES), f32)],
        compiler_params=params,
        cost_estimate=pl.CostEstimate(
            flops=flops,
            bytes_accessed=weight_bytes + n_e * group_rows * width * 10,
            transcendentals=n_e * group_rows * FF,
        ),
    )(place, arrived, cot_group, expert_full)
    back, inner_grad, activation, result_grad = pl.pallas_call(
        functools.partial(experts_backward, experts, local_count),
        grid=(n_e, chunks),
        out_shape=[
            shape((group_rows, width + LANES), bf16),
            shape((n_e, group_rows, 2 * FF), bf16),
            shape((n_e, group_rows, FF), bf16),
            shape((n_e, group_rows, width), bf16),
        ],
        in_specs=[
            scalar,
            pl.BlockSpec((count, LANES), lambda k, i: (i, width // LANES)),
            cot_spec,
            w_spec,
            inner_spec,
            dots_spec,
        ],
        out_specs=[
            rows_spec,
            inner_spec,
            pl.BlockSpec((1, count, FF), lambda k, i: (k, i, 0)),
            pl.BlockSpec((1, count, width), lambda k, i: (k, i, 0)),
        ],
        scratch_shapes=[pltpu.VMEM((group_rows, width), f32)],
        compiler_params=params,
        cost_estimate=pl.CostEstimate(
            flops=flops,
            bytes_accessed=weight_bytes + n_e * group_rows * width * 13,
            transcendentals=n_e * group_rows * FF,
        ),
    )(place, arrived, cot_group, expert_full, inner, dots)
    part = min(256, width)
    grads = pl.pallas_call(
        experts_weights,
        grid=(n_e, width // part),
        out_shape=shape((n_e, width, 3 * FF), bf16),
        in_specs=[
            pl.BlockSpec((group_rows, part), lambda k, j: (0, j)),
            pl.BlockSpec((1, group_rows, 2 * FF), lambda k, j: (k, 0, 0)),
            pl.BlockSpec((1, group_rows, part), lambda k, j: (k, 0, j)),
            pl.BlockSpec((1, group_rows, FF), lambda k, j: (k, 0, 0)),
        ],
        out_specs=pl.BlockSpec((1, part, 3 * FF), lambda k, j: (k, j, 0)),
        compiler_params=params,
        cost_estimate=pl.CostEstimate(
            flops=flops,
            bytes_accessed=weight_bytes + n_e * group_rows * width * 7,
            transcendentals=0,
        ),
    )(arrived, inner_grad, result_grad, activation)
    return out, back, grads


def body(
    tokens,
    cotangent,
    doc_lengths,
    routes,
    qkv_weight,
    qkv_mean,
    qkv_square,
    out_weight,
    out_mean,
    out_square,
    router_weight,
    router_mean,
    router_square,
    norm_gains,
    gains_mean,
    gains_square,
    in_weight,
    in_mean,
    in_square,
    down_weight,
    down_mean,
    down_square,
):
    f32, bf16 = jnp.float32, jnp.bfloat16
    shape = jax.ShapeDtypeStruct
    n_a, n_r, n_c, n_e = (lax.axis_size(name) for name in ("a", "r", "core", "exp"))
    rows, width = tokens.shape
    experts = router_weight.shape[1]
    local_count = in_weight.shape[0]
    sizes = (n_a, n_r, n_c, n_e, width // (n_a * n_r * n_c * n_e))
    home, dense, expert = (order_of(kind, sizes) for kind in ("home", "dense", "expert"))
    query_width = QUERY_HEADS * HEAD_DIMENSION
    qkv_width = query_width + 2 * KEY_VALUE_HEADS * HEAD_DIMENSION

    local_rows = qkv_weight.shape[0]
    extra = jnp.zeros((local_rows, LANES - experts - 2), bf16)
    pack = jnp.concatenate(
        [
            qkv_weight.astype(bf16),
            out_weight.astype(bf16),
            router_weight.astype(bf16),
            norm_gains.astype(bf16),
            extra,
        ],
        axis=1,
    )
    pack = spread(pack, "a")
    cot_expert = dot_nn(cotangent, reorder_matrix(home, expert)).astype(bf16)
    cot_group = lax.all_gather(cot_expert, ("core", "a"), axis=0, tiled=True)
    expert_pack = jnp.concatenate([in_weight.astype(bf16), down_weight.astype(bf16)], axis=2)
    pack, expert_pack = lax.optimization_barrier((pack, expert_pack))
    expert_pack = exchange(expert_pack, ("core", "a"))
    expert_full = lax.all_gather(expert_pack, ("exp", "r"), axis=0, tiled=True).reshape(
        n_e, width, 3 * FF
    )
    dense_full = spread(spread(pack, ("r", "exp")), "core")

    to_dense = reorder_matrix(home, dense)
    x_dense = dot_nn(tokens, to_dense).astype(bf16)
    cot_dense = dot_nn(cotangent, to_dense).astype(bf16)
    positions, segment = doc_layout(doc_lengths.reshape(-1), rows)
    cosine, sine = rope_tables(positions, HEAD_DIMENSION)
    repeat = LANES // HEAD_DIMENSION
    cosine = jnp.concatenate([cosine, cosine] * repeat, axis=1)
    sine = jnp.concatenate([-sine, sine] * repeat, axis=1)
    row_index = jnp.arange(rows, dtype=jnp.int32)
    allowed = (segment[:, None] == segment[None, :]) & (row_index[None, :] <= row_index[:, None])
    allowed = allowed.astype(f32)
    used = jnp.any(
        routes[:, :, None] == jnp.arange(LANES, dtype=jnp.int32)[None, None, :], axis=1
    ).astype(f32)
    hidden, normed, qkv, logs, attended, second, gates, sent = whole_call(
        functools.partial(attention_forward, experts, n_a),
        [
            shape((rows, width), f32),
            shape((rows, width), bf16),
            shape((rows, qkv_width), bf16),
            shape((rows, LANES), f32),
            shape((rows, query_width), bf16),
            shape((rows, width), bf16),
            shape((rows, LANES), f32),
            shape((n_a, rows, width + LANES), bf16),
        ],
        [x_dense, dense_full, cosine, sine, allowed, used, reorder_matrix(dense, expert)],
        flops=2 * rows * width * (qkv_width + 2 * width + 2 * rows),
    )

    arrived = exchange(sent, "a").reshape(n_a * rows, width + LANES)
    arrived = spread(arrived, "core")
    place = (lax.axis_index("core") * n_a + lax.axis_index("a")).astype(jnp.int32).reshape(1)
    out, back, expert_grad = run_experts(
        place, arrived, cot_group, expert_full, experts, local_count
    )
    out = exchange(collect(out, "core").astype(bf16).reshape(n_a, rows, width), "a")
    back = exchange(collect(back, "core").astype(bf16).reshape(n_a, rows, width + LANES), "a")

    from_expert = reorder_matrix(expert, dense)
    hidden_grad, branch_grad, out_grad = whole_call(
        functools.partial(home_backward, experts),
        [
            shape((rows, width), f32),
            shape((rows, width), bf16),
            shape((width, query_width + LANES), bf16),
        ],
        [back, from_expert, cot_dense, hidden, second, gates, dense_full, attended],
        flops=2 * rows * width * (n_a * width + query_width),
    )
    out_total = reduce_dense(out_grad)
    qkv_grad, input_grad = whole_call(
        functools.partial(attention_backward, experts),
        [shape((width, qkv_width + LANES), bf16), shape((rows, width), bf16)],
        [
            branch_grad,
            hidden_grad,
            dense_full,
            qkv,
            logs,
            normed,
            x_dense,
            cosine,
            sine,
            allowed,
        ],
        flops=2 * rows * width * (2 * qkv_width + width + 4 * rows),
        scratch=[pltpu.VMEM((rows, query_width), bf16), pltpu.VMEM((rows, qkv_width), bf16)],
    )
    qkv_total = reduce_dense(qkv_grad)

    expert_grad = expert_grad.reshape(
        n_e * n_r * n_c * n_a, width // (n_r * n_c * n_a), 3 * FF
    )
    expert_grad = exchange(collect(expert_grad, ("exp", "r")).astype(bf16), ("core", "a"))
    expert_grad = expert_grad.astype(f32)
    d_in = expert_grad[:, :, : 2 * FF]
    d_down = expert_grad[:, :, 2 * FF :]

    from_dense = reorder_matrix(dense, home)
    mixed = dot_nn(out[0], from_expert)
    for index in range(1, n_a):
        mixed = mixed + dot_nn(out[index], from_expert)
    block_out = dot_nn((hidden + mixed).astype(bf16), from_dense).astype(bf16)
    input_grad = dot_nn(input_grad, from_dense).astype(bf16)
    d_out = out_total[:, :query_width]
    d_router = out_total[:, query_width : query_width + experts]
    d_qkv = qkv_total[:, :qkv_width]
    d_gains = jnp.concatenate(
        [
            qkv_total[:, qkv_width : qkv_width + 1],
            out_total[:, query_width + experts : query_width + experts + 1],
        ],
        axis=1,
    )
    new_qkv, new_qkv_mean, new_qkv_square = adamw(
        qkv_weight, d_qkv, qkv_mean, qkv_square, 0.15, decay_rate
    )
    new_out, new_out_mean, new_out_square = adamw(
        out_weight, d_out, out_mean, out_square, 0.3, decay_rate
    )
    new_router, new_router_mean, new_router_square = adamw(
        router_weight, d_router, router_mean, router_square, 0.05, decay_rate
    )
    new_gains, new_gains_mean, new_gains_square = adamw(
        norm_gains, d_gains, gains_mean, gains_square, 0.8, 0.0
    )
    new_in, new_in_mean, new_in_square = adamw(in_weight, d_in, in_mean, in_square, 0.1, decay_rate)
    new_down, new_down_mean, new_down_square = adamw(
        down_weight, d_down, down_mean, down_square, 1.0, decay_rate
    )
    return (
        block_out,
        input_grad,
        new_qkv,
        new_qkv_mean,
        new_qkv_square,
        new_out,
        new_out_mean,
        new_out_square,
        new_router,
        new_router_mean,
        new_router_square,
        new_gains,
        new_gains_mean,
        new_gains_square,
        new_in,
        new_in_mean,
        new_in_square,
        new_down,
        new_down_mean,
        new_down_square,
    )


def solution(mesh):
    n_dp, n_exp = mesh.shape["dp"], mesh.shape["exp"]
    n_a = EXPERTS // n_exp // 2
    mesh = Mesh(
        mesh.devices.reshape(n_a, n_dp // (2 * n_a), 2, n_exp), ("a", "r", "core", "exp")
    )
    placed = (
        P(("a", "r", "core", "exp"), None),
        P(("a", "r", "core", "exp"), None),
        P(("a", "r", "core", "exp"), None),
        P(("a", "r", "core", "exp"), None),
        P(("a", "r", "core", "exp"), None),
        P(("a", "r", "core", "exp"), None),
        P(("a", "r", "core", "exp"), None),
        P(("a", "r", "core", "exp"), None),
        P(("a", "r", "core", "exp"), None),
        P(("a", "r", "core", "exp"), None),
        P(("a", "r", "core", "exp"), None),
        P(("a", "r", "core", "exp"), None),
        P(("a", "r", "core", "exp"), None),
        P(("a", "r", "core", "exp"), None),
        P(("a", "r", "core", "exp"), None),
        P(("a", "r", "core", "exp"), None),
        P("exp", ("a", "r", "core"), None),
        P("exp", ("a", "r", "core"), None),
        P("exp", ("a", "r", "core"), None),
        P("exp", ("a", "r", "core"), None),
        P("exp", ("a", "r", "core"), None),
        P("exp", ("a", "r", "core"), None),
    )
    return jax.shard_map(
        body,
        mesh=mesh,
        in_specs=placed,
        out_specs=(
            P(("a", "r", "core", "exp"), None),
            P(("a", "r", "core", "exp"), None),
            P(("a", "r", "core", "exp"), None),
            P(("a", "r", "core", "exp"), None),
            P(("a", "r", "core", "exp"), None),
            P(("a", "r", "core", "exp"), None),
            P(("a", "r", "core", "exp"), None),
            P(("a", "r", "core", "exp"), None),
            P(("a", "r", "core", "exp"), None),
            P(("a", "r", "core", "exp"), None),
            P(("a", "r", "core", "exp"), None),
            P(("a", "r", "core", "exp"), None),
            P(("a", "r", "core", "exp"), None),
            P(("a", "r", "core", "exp"), None),
            P("exp", ("a", "r", "core"), None),
            P("exp", ("a", "r", "core"), None),
            P("exp", ("a", "r", "core"), None),
            P("exp", ("a", "r", "core"), None),
            P("exp", ("a", "r", "core"), None),
            P("exp", ("a", "r", "core"), None),
        ),
        check_vma=False,
    )
```

time: 647 us -> 595 us (0.920)
  matrix products: 93.7 us -> 14.6 us
  Pallas kernels: 0 us -> 78.8 us
  waiting for transfers between devices: 216 us -> 273 us
  blocking collectives: 127 us -> 77.3 us
  local copies, waits for them, and re-layouts: 71.5 us -> 29.1 us
  other arithmetic: 58.4 us -> 39.5 us
    dot_general x34 -> x8, matrix products: 93.7 us -> 14.6 us  [dot_nn(): return jnp.dot(left, right, preferred_element_type=jnp.float32)]
    pallas_call x0 -> x6, Pallas kernels: none -> 78.8 us  [the longest x3 31.3 us: whole_call(): pl.pallas_call(kernel, out_shape=outputs, in_specs=[pl.BlockSpec(memory_s...]
    all_to_all x13, waiting for transfers between devices: 216 us -> 273 us  [exchange(): return lax.all_to_all(values, axes, split_axis=0, concat_axis=0, tiled=True)]
    all_to_all x6 -> x5, blocking collectives: 127 us -> 77.3 us  [exchange(): return lax.all_to_all(values, axes, split_axis=0, concat_axis=0, tiled=True)]
    reduce_sum x15 -> x1, other arithmetic: 23.6 us -> 0.09 us  [doc_layout(): segment = jnp.sum(passed, axis=1, dtype=jnp.int32)]
    concatenate x6 -> x1, local copies, waits for them, and re-layouts: 15.6 us -> 0.1 us  [body(): jnp.concatenate([qkv_weight.astype(bf16), out_weight.astype(bf16), router...]
    unnamed x221 -> x131, local copies, waits for them, and re-layouts: 7.33 us -> 20.5 us
    all_to_all x3 -> x0, local copies, waits for them, and re-layouts: 11.8 us -> none  [spread(): return lax.all_to_all(copies, axes, split_axis=0, concat_axis=0, tiled=True)]
  transfers between devices with their start and end apart: 15 -> 15, of which waited for: 10 -> 13; matrix products, arithmetic and copies ran while one was open for 22% -> 9% of each run, Pallas kernels for 0% -> 6%
where the time goes in v2:
time: 595 us; the launch traced here: 585 us
  waiting for transfers between devices  273 us (46%)
  Pallas kernels  78.8 us (13%)
  blocking collectives  77.3 us (13%)
  starting transfers between devices  58.1 us (10%)
  other arithmetic  39.5 us (7%)
  local copies, waits for them, and re-layouts  29.1 us (5%)
  between operations  15.2 us (3%)
  matrix products  14.6 us (2%)
    all_to_all x13, waiting for transfers between devices, exchange(): return lax.all_to_all(values, axes, split_axis=0, concat_axis=0, tiled=True)  273 us
    all_to_all x5, blocking collectives, exchange(): return lax.all_to_all(values, axes, split_axis=0, concat_axis=0, tiled=True)  77.3 us
    all_to_all x13, starting transfers between devices, exchange(): return lax.all_to_all(values, axes, split_axis=0, concat_axis=0, tiled=True)  58 us
    pallas_call x3, Pallas kernels, whole_call(): pl.pallas_call(kernel, out_shape=outputs, in_specs=[pl.BlockSpec(memory_s...  31.3 us
    unnamed x131, local copies, waits for them, and re-layouts  20.5 us
    pallas_call x1, Pallas kernels, run_experts(): pl.pallas_call(functools.partial(experts_backward, experts, local_count),...  17.8 us
    pallas_call x1, Pallas kernels, run_experts(): pl.pallas_call(functools.partial(experts_forward, experts, local_count),...  16.3 us
    dot_general x8, matrix products, dot_nn(): return jnp.dot(left, right, preferred_element_type=jnp.float32)  14.6 us
  transfers between devices with their start and end apart: 15, of which 13 were waited for; matrix products, arithmetic and copies ran while one was open for 9% of the time, Pallas kernels for 6%

profile of v2, /device:TPU:0, one launch (start us, length us, event | category | flops | bytes accessed | tf_op | source)
XLA Modules:
  0.0 585.1 jit_solution(16220300936736779846)
XLA Ops:
  11.8 6.4 %all-to-all-start = ((bf16[4,32,3200]{2,1,0:T(8,128)(2,1)}), bf16[4,32,3200]{2,1,0:T(8,128)(2,1)}, u32[]{:S(2)}, u32[]{:S(2)}) async-start(bf16[4,32,3200]{2,1,0:T(8,128)(2,1)} %broadcast_in_dim.15), calls=%async_computation | async-start | bytes 1638400 | tf_op jit(solution)/shard_map/all_to_all | solution.py:443
  20.2 30.2 %all-to-all-done = bf16[4,32,3200]{2,1,0:T(8,128)(2,1)} async-done(((bf16[4,32,3200]{2,1,0:T(8,128)(2,1)}), bf16[4,32,3200]{2,1,0:T(8,128)(2,1)}, u32[]{:S(2)}, u32[]{:S(2)}) %all-to-all-start) | async-done | bytes 819232 | tf_op jit(solution)/shard_map/all_to_all | solution.py:443
  50.4 40.6 %all_to_all.90 = bf16[8,64,1536]{2,1,0:T(8,128)(2,1)} all-to-all(bf16[8,64,1536]{2,1,0:T(8,128)(2,1)S(1)} %pad_maximum_fusion), channel_id=1, replica_groups=mesh['a'=4,'r'=2,'core'=2,'exp'=2] {'core','a'}, dimensions={0} | all-to-all | bytes 3145728 | tf_op jit(solution)/shard_map/all_to_all | solution.py:443
  94.1 5.0 all-to-all-start.1
  103.3 50.2 %all-to-all-done.1 = bf16[4,128,3200]{2,1,0:T(8,128)(2,1)} async-done(((bf16[4,128,3200]{2,1,0:T(8,128)(2,1)}), bf16[4,128,3200]{2,1,0:T(8,128)(2,1)}, u32[]{:S(2)}, u32[]{:S(2)}) %all-to-all-start.1) | async-done | bytes 3276832 | tf_op jit(solution)/shard_map/all_to_all | solution.py:443
  155.8 10.5 %all_to_all.91 = bf16[2,512,3200]{2,1,0:T(8,128)(2,1)} all-to-all(bf16[2,512,3200]{2,1,0:T(8,128)(2,1)S(1)} %broadcast_in_dim.18), channel_id=1, replica_groups=mesh['a'=4,'r'=2,'core'=2,'exp'=2] {'core'}, dimensions={0} | all-to-all | bytes 13107200 | tf_op jit(solution)/shard_map/all_to_all | solution.py:443
  166.4 11.3 %shard_map.392 = (f32[128,1024]{1,0:T(8,128)S(1)}, bf16[128,1024]{1,0:T(8,128)(2,1)S(1)}, bf16[128,2048]{1,0:T(8,128)(2,1)S(1)}, f32[128,128]{1,0:T(8,128)S(1)},...) custom-call(bf16[128,1024]{1,0:T(8,128)(2,1)S(1)} %fusion.49.x_ref, ...), custom_call_target="tpu_custom_call" | custom-call | flops 1140850688 | bytes 12320768 | tf_op jit(solution)/shard_map/pallas_call | solution.py:422
  186.2 29.1 %all-to-all-done.3 = bf16[4,128,1152]{2,1,0:T(8,128)(2,1)S(1)} async-done(((bf16[4,128,1152]{2,1,0:T(8,128)(2,1)}), bf16[4,128,1152]{2,1,0:T(8,128)(2,1)S(1)}, u32[]{:S(2)}, u32[]{:S(2)}) %all-to-all-start.3) | async-done | bytes 1179680 | tf_op jit(solution)/shard_map/all_to_all | solution.py:443
  216.8 5.1 all-to-all-start.4
  226.6 16.3 %shard_map.393 = (bf16[1024,1024]{1,0:T(8,128)(2,1)}, bf16[1024,128]{1,0:T(8,128)(2,1)S(1)}, f32[2,1024,1024]{2,1,0:T(8,128)}) custom-call(s32[1]{0:T(128)} %bitcast.5.place_ref, bf16[1024,1152]{1,0:T(8,128)(2,1)} %bitcast.7.rows_ref.gates_ref, bf16[1024,1024]{1,0:T(8,128)(2,1)S(1)} %copy-done.31, bf16[2,1024,1536]{2,1,0:T(8,128)(2,1)} %bitcast.61), custom_call_target="tpu_custom_call" | custom-call | flops 6442450944 | bytes 27262976 | tf_op jit(solution)/shard_map/pallas_call | solution.py:483
  242.9 17.8 %shard_map.394 = (bf16[1024,1152]{1,0:T(8,128)(2,1)}, bf16[2,1024,1024]{2,1,0:T(8,128)(2,1)}, bf16[2,1024,512]{2,1,0:T(8,128)(2,1)S(1)}, bf16[2,1024,1024]{2,1,0:T(8,128)(2,1)}) custom-call(s32[1]{0:T(128)} %bitcast.5.place_ref, bf16[1024,1152]{1,0:T(8,128)(2,1)} %bitcast.7.rows_ref.gates_ref, bf16[1024,1024]{1,0:T(8,128)(2,1)S(1)} %copy-done.31, ...), custom_call_target="tpu_custom_call" | custom-call | flops 6442450944 | bytes 33554432 | tf_op jit(solution)/shard_map/pallas_call | solution.py:501
  260.7 6.8 %all_to_all.92 = bf16[2,512,1152]{2,1,0:T(8,128)(2,1)S(1)} all-to-all(bf16[2,512,1152]{2,1,0:T(8,128)(2,1)} %bitcast.58), channel_id=1, replica_groups=mesh['a'=4,'r'=2,'core'=2,'exp'=2] {'core'}, dimensions={0} | all-to-all | bytes 4718592 | tf_op jit(solution)/shard_map/all_to_all | solution.py:443
  273.9 27.5 %all-to-all-done.9.parts_ref = bf16[4,128,1152]{2,1,0:T(8,128)(2,1)S(1)} async-done(((bf16[4,128,1152]{2,1,0:T(8,128)(2,1)}), bf16[4,128,1152]{2,1,0:T(8,128)(2,1)S(1)}, u32[]{:S(2)}, u32[]{:S(2)}) %all-to-all-start.9) | async-done | bytes 1179680 | tf_op jit(solution)/shard_map/all_to_all | solution.py:443
  306.2 6.8 %shard_map.395 = (f32[128,1024]{1,0:T(8,128)S(1)}, bf16[128,1024]{1,0:T(8,128)(2,1)S(1)}, bf16[1024,1152]{1,0:T(8,128)(2,1)}) custom-call(bf16[4,128,1152]{2,1,0:T(8,128)(2,1)S(1)} %all-to-all-done.9.parts_ref, bf16[1024,1024]{1,0:T(8,128)(2,1)S(1)} %get-tuple-element.208.order_ref, bf16[128,1024]{1,0:T(8,128)(2,1)S(1)} %copy-done.26, ...), custom_call_target="tpu_custom_call" | custom-call | flops 1342177280 | bytes 14352384 | tf_op jit(solution)/shard_map/pallas_call | solution.py:422
  313.0 6.8 %all_to_all.93 = bf16[2,512,1152]{2,1,0:T(8,128)(2,1)S(1)} all-to-all(bf16[2,512,1152]{2,1,0:T(8,128)(2,1)} %bitcast.59), channel_id=1, replica_groups=mesh['a'=4,'r'=2,'core'=2,'exp'=2] {'core'}, dimensions={0} | all-to-all | bytes 4718592 | tf_op jit(solution)/shard_map/all_to_all | solution.py:443
  319.9 4.8 all-to-all-start.6
  334.4 12.4 %all-to-all-done.14 = bf16[4,128,1152]{2,1,0:T(8,128)(2,1)S(1)} async-done(((bf16[4,128,1152]{2,1,0:T(8,128)(2,1)}), bf16[4,128,1152]{2,1,0:T(8,128)(2,1)S(1)}, u32[]{:S(2)}, u32[]{:S(2)}) %all-to-all-start.14) | async-done | bytes 1179680 | tf_op jit(solution)/shard_map/all_to_all | solution.py:443
  346.8 4.5 all-to-all-start.7
  351.4 13.2 %shard_map.396 = (bf16[1024,2176]{1,0:T(8,128)(2,1)}, bf16[128,1024]{1,0:T(8,128)(2,1)S(1)}) custom-call(bf16[128,1024]{1,0:T(8,128)(2,1)S(1)} %copy-done.25, f32[128,1024]{1,0:T(8,128)S(1)} %copy-done.17, bf16[1024,3200]{1,0:T(8,128)(2,1)} %bitcast.50, bf16[128,2048]{1,0:T(8,128)(2,1)S(1)} %copy-done.15, f32[128,128]{1,0:T(8,128)S(1)} %copy-done.28, ...), custom_call_target="tpu_custom_call" | custom-call | flops 1476395008 | bytes 13369344 | tf_op jit(solution)/shard_map/pallas_call | solution.py:422
  365.5 11.4 %all-to-all-done.7 = bf16[4,128,1024]{2,1,0:T(8,128)(2,1)} async-done(((bf16[4,128,1024]{2,1,0:T(8,128)(2,1)}), bf16[4,128,1024]{2,1,0:T(8,128)(2,1)}, u32[]{:S(2)}, u32[]{:S(2)}) %all-to-all-start.7) | async-done | bytes 1048608 | tf_op jit(solution)/shard_map/all_to_all | solution.py:443
  376.8 12.4 %all_to_all.94 = bf16[2,512,2176]{2,1,0:T(8,128)(2,1)} all-to-all(bf16[2,512,2176]{2,1,0:T(8,128)(2,1)} %bitcast.56), channel_id=1, replica_groups=mesh['a'=4,'r'=2,'core'=2,'exp'=2] {'core'}, dimensions={0} | all-to-all | bytes 8912896 | tf_op jit(solution)/shard_map/all_to_all | solution.py:443
  392.7 4.2 add_convert_fusion
  396.9 5.9 %all-to-all-done.15 = bf16[4,32,1152]{2,1,0:T(8,128)(2,1)S(1)} async-done(((bf16[4,32,1152]{2,1,0:T(8,128)(2,1)}), bf16[4,32,1152]{2,1,0:T(8,128)(2,1)S(1)}, u32[]{:S(2)}, u32[]{:S(2)}) %all-to-all-start.15) | async-done | bytes 294944 | tf_op jit(solution)/shard_map/all_to_all | solution.py:443
  403.5 4.6 all-to-all-start.11
  408.1 13.4 %shard_map.397 = bf16[2,1024,1536]{2,1,0:T(8,128)(2,1)} custom-call(bf16[1024,1152]{1,0:T(8,128)(2,1)} %bitcast.7.rows_ref.gates_ref, bf16[2,1024,1024]{2,1,0:T(8,128)(2,1)} %get-tuple-element.61.inner_grad_ref, bf16[2,1024,1024]{2,1,0:T(8,128)(2,1)} %get-tuple-element.62.result_grad_ref, bf16[2,1024,512]{2,1,0:T(8,128)(2,1)S(1)} %copy-done.33), custom_call_target="tpu_custom_call" | custom-call | flops 6442450944 | bytes 20971520 | tf_op jit(solution)/shard_map/pallas_call | solution.py:533
  421.5 11.9 %all-to-all-done.11 = bf16[4,128,2176]{2,1,0:T(8,128)(2,1)} async-done(((bf16[4,128,2176]{2,1,0:T(8,128)(2,1)}), bf16[4,128,2176]{2,1,0:T(8,128)(2,1)}, u32[]{:S(2)}, u32[]{:S(2)}) %all-to-all-start.11) | async-done | bytes 2228256 | tf_op jit(solution)/shard_map/all_to_all | solution.py:443
  433.5 5.4 all-to-all-start.16
  447.8 60.6 %all-to-all-done.16 = bf16[4,8,64,1536]{3,2,1,0:T(8,128)(2,1)} async-done(((bf16[4,8,64,1536]{3,2,1,0:T(8,128)(2,1)}), bf16[4,8,64,1536]{3,2,1,0:T(8,128)(2,1)}, u32[]{:S(2)}, u32[]{:S(2)}) %all-to-all-start.16) | async-done | bytes 6291488 | tf_op jit(solution)/shard_map/all_to_all | solution.py:443
  517.5 4.8 fusion.27
  526.1 4.3 all-to-all-start.17
  543.1 24.6 %all-to-all-done.17 = bf16[8,64,1536]{2,1,0:T(8,128)(2,1)} async-done(((bf16[8,64,1536]{2,1,0:T(8,128)(2,1)}), bf16[8,64,1536]{2,1,0:T(8,128)(2,1)}, u32[]{:S(2)}, u32[]{:S(2)}) %all-to-all-start.17) | async-done | bytes 1572896 | tf_op jit(solution)/shard_map/all_to_all | solution.py:443
  569.9 5.7 multiply_subtract_fusion
  (197 shorter events, 95.1 us)
Async XLA Ops:
  7.2 11.0 %copy-start = (bf16[128,1024]{1,0:T(8,128)(2,1)S(1)}, bf16[128,1024]{1,0:T(8,128)(2,1)}, u32[]{:S(2)}) copy-start(bf16[128,1024]{1,0:T(8,128)(2,1)} %param.26) | copy-start | bytes 786436
  7.2 11.0 %copy-start.51 = (s32[1024]{0:T(1024)S(1)}, s32[1024]{0:T(1024)}, u32[]{:S(2)}) copy-start(s32[1024]{0:T(1024)} %constant.40.clone) | copy-start | bytes 12292
  11.8 38.7 %all-to-all-start = ((bf16[4,32,3200]{2,1,0:T(8,128)(2,1)}), bf16[4,32,3200]{2,1,0:T(8,128)(2,1)}, u32[]{:S(2)}, u32[]{:S(2)}) async-start(bf16[4,32,3200]{2,1,0:T(8,128)(2,1)} %broadcast_in_dim.15), calls=%async_computation | async-start | bytes 1638400 | tf_op jit(solution)/shard_map/all_to_all | solution.py:443
  18.2 203.7 %all-gather.3.cloned.1.call-start = ((), (), s32[]{:S(2)}) async-start(), calls=%async_computation.18 | async-start | bytes 2359296 | tf_op jit(solution)/shard_map/all_gather | solution.py:603
  19.8 205.2 %all-gather.5.cloned.1.call-start = ((), (), s32[]{:S(2)}) async-start(), calls=%async_computation.19 | async-start | bytes 7864320 | tf_op jit(solution)/shard_map/all_gather | solution.py:607
  94.1 59.3 %all-to-all-start.1 = ((bf16[4,128,3200]{2,1,0:T(8,128)(2,1)}), bf16[4,128,3200]{2,1,0:T(8,128)(2,1)}, u32[]{:S(2)}, u32[]{:S(2)}) async-start(bf16[4,128,3200]{2,1,0:T(8,128)(2,1)} %broadcast_in_dim.16), calls=%async_computation.1 | async-start | bytes 6553600 | tf_op jit(solution)/shard_map/all_to_all | solution.py:443
  100.4 65.9 %copy-start.5 = (f32[128,128]{1,0:T(8,128)}, f32[128,128]{1,0:T(8,128)S(1)}, u32[]{:S(2)}) copy-start(f32[128,128]{1,0:T(8,128)S(1)} %get-tuple-element.213.cos_ref) | copy-start | bytes 196612
  100.5 65.9 %copy-start.7 = (f32[128,128]{1,0:T(8,128)}, f32[128,128]{1,0:T(8,128)S(1)}, u32[]{:S(2)}) copy-start(f32[128,128]{1,0:T(8,128)S(1)} %get-tuple-element.214.sin_ref) | copy-start | bytes 196612
  100.6 65.8 %copy-start.9 = (f32[128,128]{1,0:T(8,128)}, f32[128,128]{1,0:T(8,128)S(1)}, u32[]{:S(2)}) copy-start(f32[128,128]{1,0:T(8,128)S(1)} %fusion.58.allow_ref) | copy-start | bytes 196612
  101.4 65.0 %copy-start.3 = (bf16[128,1024]{1,0:T(8,128)(2,1)}, bf16[128,1024]{1,0:T(8,128)(2,1)S(1)}, u32[]{:S(2)}) copy-start(bf16[128,1024]{1,0:T(8,128)(2,1)S(1)} %fusion.49.x_ref) | copy-start | bytes 786436
  182.7 32.6 %all-to-all-start.3 = ((bf16[4,128,1152]{2,1,0:T(8,128)(2,1)}), bf16[4,128,1152]{2,1,0:T(8,128)(2,1)S(1)}, u32[]{:S(2)}, u32[]{:S(2)}) async-start(bf16[4,128,1152]{2,1,0:T(8,128)(2,1)} %get-tuple-element.44), calls=%async_computation.3 | async-start | bytes 2359296 | tf_op jit(solution)/shard_map/all_to_all | solution.py:443
  216.8 8.2 %all-to-all-start.4 = ((bf16[2,512,1152]{2,1,0:T(8,128)(2,1)}), bf16[2,512,1152]{2,1,0:T(8,128)(2,1)}, u32[]{:S(2)}, u32[]{:S(2)}) async-start(bf16[2,512,1152]{2,1,0:T(8,128)(2,1)} %broadcast_in_dim.20), calls=%async_computation.4 | async-start | bytes 4718592 | tf_op jit(solution)/shard_map/all_to_all | solution.py:443
  268.8 32.6 %all-to-all-start.9 = ((bf16[4,128,1152]{2,1,0:T(8,128)(2,1)}), bf16[4,128,1152]{2,1,0:T(8,128)(2,1)S(1)}, u32[]{:S(2)}, u32[]{:S(2)}) async-start(bf16[4,128,1152]{2,1,0:T(8,128)(2,1)} %bitcast.55), calls=%async_computation.9 | async-start | bytes 2359296 | tf_op jit(solution)/shard_map/all_to_all | solution.py:443
  319.9 7.8 %all-to-all-start.6 = ((bf16[2,512,1024]{2,1,0:T(8,128)(2,1)}), bf16[2,512,1024]{2,1,0:T(8,128)(2,1)}, u32[]{:S(2)}, u32[]{:S(2)}) async-start(bf16[2,512,1024]{2,1,0:T(8,128)(2,1)} %bitcast.10), calls=%async_computation.6 | async-start | bytes 4194304 | tf_op jit(solution)/shard_map/all_to_all | solution.py:443
  327.7 19.1 %all-to-all-start.14 = ((bf16[4,128,1152]{2,1,0:T(8,128)(2,1)}), bf16[4,128,1152]{2,1,0:T(8,128)(2,1)S(1)}, u32[]{:S(2)}, u32[]{:S(2)}) async-start(bf16[4,128,1152]{2,1,0:T(8,128)(2,1)} %bitcast.54), calls=%async_computation.14 | async-start | bytes 2359296 | tf_op jit(solution)/shard_map/all_to_all | solution.py:443
  331.2 20.1 %copy-start.4 = (bf16[128,1024]{1,0:T(8,128)(2,1)S(1)}, bf16[128,1024]{1,0:T(8,128)(2,1)}, u32[]{:S(2)}) copy-start(bf16[128,1024]{1,0:T(8,128)(2,1)} %copy-done.3) | copy-start | bytes 786436
  331.2 20.1 %copy-start.6 = (f32[128,128]{1,0:T(8,128)S(1)}, f32[128,128]{1,0:T(8,128)}, u32[]{:S(2)}) copy-start(f32[128,128]{1,0:T(8,128)} %copy-done.5) | copy-start | bytes 196612
  331.2 20.1 %copy-start.8 = (f32[128,128]{1,0:T(8,128)S(1)}, f32[128,128]{1,0:T(8,128)}, u32[]{:S(2)}) copy-start(f32[128,128]{1,0:T(8,128)} %copy-done.7) | copy-start | bytes 196612
  331.2 20.1 %copy-start.10 = (f32[128,128]{1,0:T(8,128)S(1)}, f32[128,128]{1,0:T(8,128)}, u32[]{:S(2)}) copy-start(f32[128,128]{1,0:T(8,128)} %copy-done.9) | copy-start | bytes 196612
  331.2 20.1 %copy-start.15 = (bf16[128,2048]{1,0:T(8,128)(2,1)S(1)}, bf16[128,2048]{1,0:T(8,128)(2,1)}, u32[]{:S(2)}) copy-start(bf16[128,2048]{1,0:T(8,128)(2,1)} %copy-done.14) | copy-start | bytes 1572868
  331.3 20.1 %copy-start.17 = (f32[128,1024]{1,0:T(8,128)S(1)}, f32[128,1024]{1,0:T(8,128)}, u32[]{:S(2)}) copy-start(f32[128,1024]{1,0:T(8,128)} %copy-done.16) | copy-start | bytes 1572868
  331.3 20.1 %copy-start.19 = (bf16[128,1024]{1,0:T(8,128)(2,1)S(1)}, bf16[128,1024]{1,0:T(8,128)(2,1)}, u32[]{:S(2)}) copy-start(bf16[128,1024]{1,0:T(8,128)(2,1)} %copy-done.18) | copy-start | bytes 786436
  331.3 20.1 %copy-start.25 = (bf16[128,1024]{1,0:T(8,128)(2,1)S(1)}, bf16[128,1024]{1,0:T(8,128)(2,1)}, u32[]{:S(2)}) copy-start(bf16[128,1024]{1,0:T(8,128)(2,1)} %copy-done.24) | copy-start | bytes 786436
  331.3 20.1 %copy-start.28 = (f32[128,128]{1,0:T(8,128)S(1)}, f32[128,128]{1,0:T(8,128)}, u32[]{:S(2)}) copy-start(f32[128,128]{1,0:T(8,128)} %copy-done.27) | copy-start | bytes 196612
  346.8 30.0 %all-to-all-start.7 = ((bf16[4,128,1024]{2,1,0:T(8,128)(2,1)}), bf16[4,128,1024]{2,1,0:T(8,128)(2,1)}, u32[]{:S(2)}, u32[]{:S(2)}) async-start(bf16[4,128,1024]{2,1,0:T(8,128)(2,1)} %bitcast.57), calls=%async_computation.7 | async-start | bytes 2097152 | tf_op jit(solution)/shard_map/all_to_all | solution.py:443
  389.2 13.6 %all-to-all-start.15 = ((bf16[4,32,1152]{2,1,0:T(8,128)(2,1)}), bf16[4,32,1152]{2,1,0:T(8,128)(2,1)S(1)}, u32[]{:S(2)}, u32[]{:S(2)}) async-start(bf16[4,32,1152]{2,1,0:T(8,128)(2,1)} %bitcast.25), calls=%async_computation.15 | async-start | bytes 589824 | tf_op jit(solution)/shard_map/all_to_all | solution.py:443
  403.5 29.9 %all-to-all-start.11 = ((bf16[4,128,2176]{2,1,0:T(8,128)(2,1)}), bf16[4,128,2176]{2,1,0:T(8,128)(2,1)}, u32[]{:S(2)}, u32[]{:S(2)}) async-start(bf16[4,128,2176]{2,1,0:T(8,128)(2,1)} %bitcast.51), calls=%async_computation.11 | async-start | bytes 4456448 | tf_op jit(solution)/shard_map/all_to_all | solution.py:443
  433.5 75.0 %all-to-all-start.16 = ((bf16[4,8,64,1536]{3,2,1,0:T(8,128)(2,1)}), bf16[4,8,64,1536]{3,2,1,0:T(8,128)(2,1)}, u32[]{:S(2)}, u32[]{:S(2)}) async-start(bf16[4,8,64,1536]{3,2,1,0:T(8,128)(2,1)} %bitcast.52), calls=%async_computation.16 | async-start | bytes 12582912 | tf_op jit(solution)/shard_map/all_to_all | solution.py:443
  445.1 67.2 %copy-start.13 = (f32[128,1024]{1,0:T(8,128)S(1)}, f32[128,1024]{1,0:T(8,128)}, u32[]{:S(2)}) copy-start(f32[128,1024]{1,0:T(8,128)} %copy-done.11) | copy-start | bytes 1572868
  508.4 17.7 %all-to-all-start.12 = ((bf16[4,32,2176]{2,1,0:T(8,128)(2,1)}), bf16[4,32,2176]{2,1,0:T(8,128)(2,1)S(1)}, u32[]{:S(2)}, u32[]{:S(2)}) async-start(bf16[4,32,2176]{2,1,0:T(8,128)(2,1)} %bitcast.21), calls=%async_computation.12 | async-start | bytes 1114112 | tf_op jit(solution)/shard_map/all_to_all | solution.py:443
  526.1 41.7 %all-to-all-start.17 = ((bf16[8,64,1536]{2,1,0:T(8,128)(2,1)}), bf16[8,64,1536]{2,1,0:T(8,128)(2,1)}, u32[]{:S(2)}, u32[]{:S(2)}) async-start(bf16[8,64,1536]{2,1,0:T(8,128)(2,1)} %fusion.27), calls=%async_computation.17 | async-start | bytes 3145728 | tf_op jit(solution)/shard_map/all_to_all | solution.py:443
  543.1 26.6 %copy-start.35 = (f32[8,64,1024]{2,1,0:T(8,128)S(1)}, f32[8,64,1024]{2,1,0:T(8,128)}, u32[]{:S(2)}) copy-start(f32[8,64,1024]{2,1,0:T(8,128)} %param.41) | copy-start | bytes 6291460
  (43 other events, 185.7 us)
Sparse Core Ops, SparseCore 0:
  21.2 36.1 all-gather.2
  91.2 101.2 all-gather.4
